TPU v7x, 512 devices: a whole 4x4x16 slice. The times are simulated.
512 devices in a mesh: row: 32 (over z, core), col: 8 (over x_hi, y), dp: 2 (over x_lo).
Axes of the slice: x: 4 (x_hi: 2, x_lo: 2; x = x_hi * 2 + x_lo), y: 4, z: 16, core: 2. Of those that a mesh axis runs over, the one named last changes fastest.
Arguments:
- activations: bfloat16 [2, 1024, 25600], P('dp', 'col', 'row'), may hold values from -12 to 12
- out_grads: bfloat16 [2, 1024, 5120], P('dp', 'row', 'col'), may hold values from -12 to 12
- weight: bfloat16 [25600, 5120], P('row', 'col'), may hold values from -0.078125 to 0.078125
Outputs:
- input_grads: bfloat16 [2, 1024, 25600], P('dp', 'col', 'row')
- example_norms: float32 [2], P('dp')
- weight_grad: float32 [25600, 5120], P('row', 'col')
All inputs are finite; a program needn't handle non-finite values.
Results may differ from a plain program's by a relative error of at most 0.001.
Values may be sent and summed in bfloat16 or wider, within the bound.
No kernel may reach another device: no remote copies, remote signals or barrier semaphores. Data moves between devices by JAX's collectives and lax.ppermute only.
A program may use at most 64 MiB of HBM per device.

v0:
```python
import math

import jax
import jax.numpy as jnp
from jax import lax
from jax.sharding import PartitionSpec as P

FF = 25600
D = 5120
TOK = 1024


def local(activations, out_grads, weight):
    hidden = activations[0]
    grads = out_grads[0]
    grads_full = lax.all_gather(grads, "row", axis=0, tiled=True)
    hidden_full = lax.all_gather(hidden, "col", axis=0, tiled=True)
    input_part = lax.psum_scatter(
        jnp.einsum("td,fd->tf", grads_full, weight, preferred_element_type=jnp.float32),
        "col",
        scatter_dimension=0,
        tiled=True,
    ).astype(jnp.bfloat16)
    grad_block = jnp.einsum(
        "tf,td->fd", hidden_full, grads_full, preferred_element_type=jnp.float32
    )
    squared = lax.psum(jnp.sum(grad_block * grad_block), ("row", "col"))
    norm_value = jnp.sqrt(squared)
    bound = math.sqrt(TOK * FF * D)
    factor = 1.0 / jnp.maximum(1.0, norm_value / bound)
    weight_grad = lax.psum(factor * grad_block, "dp")
    return (input_part[None], jnp.reshape(norm_value, (1,)), weight_grad)


def solution(mesh):
    return jax.shard_map(
        local,
        mesh=mesh,
        in_specs=(P("dp", "col", "row"), P("dp", "row", "col"), P("row", "col")),
        out_specs=(P("dp", "col", "row"), P("dp"), P("row", "col")),
        check_vma=False,
    )
```

profile of v0, /device:TPU:1, one launch (start us, length us, event | category | flops | bytes accessed | tf_op | source)
XLA Modules:
  0.0 898.8 jit_solution(4459756010745923045)
XLA Ops:
  7.2 0.0 copy-start
  7.2 0.0 all-gather.5.cloned.1.call-start
  7.2 0.7 all-gather.5.cloned.1.call-update
  7.9 0.0 all-gather.7.cloned.1.call-start
  8.0 0.7 all-gather.7.cloned.1.call-update
  8.7 0.0 reduce-scatter.2.cloned.1.call-start
  8.7 78.3 %all-gather.5.cloned.1.call-done = bf16[1,1024,640]{2,1,0:T(8,128)(2,1)} async-done(((bf16[1,32,640]{2,1,0:T(8,128)(2,1)}), bf16[1,1024,640]{2,1,0:T(8,128)(2,1)}) %all-gather.5.cloned.1.call-update) | async-done | bytes 1310736 | tf_op jit(solution)/shard_map/all_gather | solution.py:16
  87.0 0.0 copy-done
  87.0 4.4 fusion.3
  91.5 0.0 reduce-scatter.2.cloned.1.call-update
  91.5 0.0 all-reduce.2.cloned.1.call-start
  91.5 60.5 %all-gather.7.cloned.1.call-done = bf16[1,1024,800]{1,2,0:T(8,128)(2,1)} async-done(((bf16[1,128,800]{1,2,0:T(8,128)(2,1)}), bf16[1,1024,800]{1,2,0:T(8,128)(2,1)}) %all-gather.7.cloned.1.call-update) | async-done | bytes 1638416 | tf_op jit(solution)/shard_map/all_gather | solution.py:17
  152.0 4.0 multiply_reduce_fusion
  156.0 635.5 %psum.14 = f32[]{:T(128)} all-reduce(f32[]{:T(128)} %get-tuple-element.3), channel_id=1, replica_groups=mesh['row'=32,'col'=8,'dp'=2] {'row','col'}, use_global_device_ids=true, to_apply=%region_2.0 | all-reduce | flops 1 | bytes 8 | tf_op jit(solution)/shard_map/psum | solution.py:27
  792.2 1.4 broadcast_multiply_fusion
  793.7 0.0 all-reduce.2.cloned.1.call-update
  793.7 0.0 reduce-scatter.2.cloned.1.call-done
  793.7 1.7 convert_bitcast_fusion
  795.4 92.7 %all-reduce.2.cloned.1.call-done = f32[800,640]{1,0:T(8,128)} async-done(((f32[800,640]{1,0:T(8,128)}), f32[800,640]{1,0:T(8,128)}) %all-reduce.2.cloned.1.call-update) | async-done | bytes 2048016 | tf_op jit(solution)/shard_map/psum | solution.py:31
  888.2 3.0 copy.7
Async XLA Ops:
  7.2 79.8 %copy-start = (bf16[800,640]{1,0:T(8,128)(2,1)S(1)}, bf16[800,640]{1,0:T(8,128)(2,1)}, u32[]{:S(2)}) copy-start(bf16[800,640]{1,0:T(8,128)(2,1)} %param.5) | copy-start | bytes 3072004
  7.2 79.8 %all-gather.5.cloned.1.call-start = ((), (), s32[]{:S(2)}) async-start(), calls=%async_computation.3 | async-start | bytes 1351680 | tf_op jit(solution)/shard_map/all_gather | solution.py:16
  7.9 144.1 %all-gather.7.cloned.1.call-start = ((), (), s32[]{:S(2)}) async-start(), calls=%async_computation.4 | async-start | bytes 1843200 | tf_op jit(solution)/shard_map/all_gather | solution.py:17
  8.7 785.0 %reduce-scatter.2.cloned.1.call-start = ((), (), s32[]{:S(2)}) async-start(), calls=%async_computation.1 | async-start | bytes 3686400 | tf_op jit(solution)/shard_map/reduce_scatter | solution.py:18
  91.5 796.7 %all-reduce.2.cloned.1.call-start = ((), (), s32[]{:S(2)}) async-start(), calls=%async_computation.2 | async-start | bytes 4096000 | tf_op jit(solution)/shard_map/psum | solution.py:31
Sparse Core Ops, SparseCore 0:
  10.1 76.8 all-gather.4
  90.1 61.9 all-gather.6
  156.7 93.3 reduce-scatter.1
  793.8 94.3 all-reduce.1
where the time goes:
time: 899 us
  blocking collectives  636 us (71%)
  waiting for transfers between devices  233 us (26%)
  between operations  15.6 us (2%)
    psum x1, blocking collectives, local(): squared = lax.psum(jnp.sum(grad_block * grad_block), ('row', 'col'))  636 us
    psum x1, waiting for transfers between devices, local(): weight_grad = lax.psum(factor * grad_block, 'dp')  92.7 us
    all_gather x1, waiting for transfers between devices, local(): grads_full = lax.all_gather(grads, 'row', axis=0, tiled=True)  78.3 us
    all_gather x1, waiting for transfers between devices, local(): hidden_full = lax.all_gather(hidden, 'col', axis=0, tiled=True)  60.5 us
  transfers between devices with their start and end apart: 4, of which 3 were waited for; matrix products, arithmetic and copies ran while one was open for 1% of the time, Pallas kernels for 0%

commit v1 on v0

v1 whole, which is shorter than its diff:
```python
import math

import jax
import jax.numpy as jnp
from jax import lax
from jax.experimental import pallas as pl
from jax.experimental.pallas import tpu as pltpu
from jax.sharding import Mesh
from jax.sharding import PartitionSpec as P

FF = 25600
D = 5120
TOK = 1024

AXES = ("za", "zb", "core", "xh", "y", "xl")
SIZES = (4, 4, 2, 2, 4, 2)
F_LOC = 800
D_LOC = 640
BF16 = jnp.bfloat16
F32 = jnp.float32
VMEM_LIMIT = 24 * 1024 * 1024


def flip(size, k):
    return [(i, i ^ k) for i in range(size)]


def dh_call(pos, mine, other, weight):
    def body(pos, mine, other, w, full, p0, p1, p2, p3):
        core, xh = pos[2], pos[3]
        for b in range(4):
            for a in range(4):
                start = ((pos[0] ^ a) * 4 + b) * 64
                here = pl.multiple_of(start + core * 32, 32)
                there = pl.multiple_of(start + (1 - core) * 32, 32)
                full[pl.ds(here, 32), :] = mine[b, a]
                full[pl.ds(there, 32), :] = other[b, a]
        weight = w[...]
        for k, out in enumerate((p0, p1, p2, p3)):
            for dx in range(2):
                start = ((xh ^ dx) * 4 + (pos[4] ^ k)) * 128
                out[dx] = lax.dot_general(
                    weight,
                    full[pl.ds(pl.multiple_of(start, 128), 128), :],
                    (((1,), (1,)), ((), ())),
                    preferred_element_type=F32,
                )

    vmem = pl.BlockSpec(memory_space=pltpu.VMEM)
    part = jax.ShapeDtypeStruct((2, F_LOC, 128), F32)
    return pl.pallas_call(
        body,
        out_shape=(jax.ShapeDtypeStruct((TOK, D_LOC), BF16),) + (part,) * 4,
        in_specs=[pl.BlockSpec(memory_space=pltpu.SMEM)] + [vmem] * 3,
        out_specs=(vmem,) * 5,
        compiler_params=pltpu.CompilerParams(vmem_limit_bytes=VMEM_LIMIT),
        cost_estimate=pl.CostEstimate(
            flops=2 * TOK * F_LOC * D_LOC, bytes_accessed=6_000_000, transcendentals=0
        ),
        name="input_grad_partials",
    )(pos, mine, other, weight)


def wg_call(hidden, full):
    def body(hidden, full, out, square):
        lhs = jnp.concatenate([hidden[j] for j in range(8)], axis=1)
        acc = jnp.dot(lhs, full[...], preferred_element_type=F32)
        out[...] = acc
        square[...] = jnp.full((8, 128), jnp.sum(acc * acc), F32)

    vmem = pl.BlockSpec(memory_space=pltpu.VMEM)
    return pl.pallas_call(
        body,
        out_shape=(
            jax.ShapeDtypeStruct((F_LOC, D_LOC), F32),
            jax.ShapeDtypeStruct((8, 128), F32),
        ),
        in_specs=[vmem] * 2,
        out_specs=(vmem,) * 2,
        compiler_params=pltpu.CompilerParams(vmem_limit_bytes=VMEM_LIMIT),
        cost_estimate=pl.CostEstimate(
            flops=2 * TOK * F_LOC * D_LOC, bytes_accessed=5_000_000, transcendentals=0
        ),
        name="weight_grad_block",
    )(hidden, full)


def local(activations, out_grads, weight):
    pos = jnp.stack([lax.axis_index(a) for a in AXES]).astype(jnp.int32)
    xl = pos[5]

    hidden = activations[0].T
    hidden_full = lax.all_to_all(
        jnp.broadcast_to(hidden[None], (8, F_LOC, 128)), ("xh", "y"), 0, 0
    )

    grads = out_grads[0]
    far = [lax.ppermute(grads, "za", flip(4, k)) for k in (1, 2, 3)]
    mine = lax.all_gather(jnp.stack([grads, *far]), "zb")
    other = lax.ppermute(mine, "core", flip(2, 1))

    full, p0, *parts = dh_call(pos, mine, other, weight)
    got = [lax.ppermute(p, "y", flip(4, k)) for k, p in zip((1, 2, 3), parts)]
    block, square = wg_call(hidden_full, full)
    peer = lax.ppermute(block, "xl", flip(2, 1))

    squared = jnp.where(jnp.arange(2) == xl, square[0, 0], 0.0)
    spread = jnp.broadcast_to(squared, (128, 2))
    squared = jnp.sum(lax.all_to_all(spread, ("za", "zb", "core", "y"), 0, 0), axis=0)
    squared, got = lax.optimization_barrier((squared, got))
    half = p0 + got[0] + got[1] + got[2]
    away = lax.ppermute(half[1], "xh", flip(2, 1))
    squared, half = lax.optimization_barrier((squared, half))
    squared = lax.psum(squared, ("xh", "xl"))
    norms = jnp.sqrt(squared)
    bound = math.sqrt(TOK * FF * D)
    factor = 1.0 / jnp.maximum(1.0, norms / bound)
    weight_grad = factor[xl] * block + factor[1 - xl] * peer

    input_grads = (half[0] + away).astype(BF16).T[None]
    return (input_grads, jnp.reshape(norms[xl], (1,)), weight_grad)


def solution(mesh):
    fine = Mesh(mesh.devices.reshape(SIZES), AXES)
    row, col = ("za", "zb", "core"), ("xh", "y")
    return jax.shard_map(
        local,
        mesh=fine,
        in_specs=(P("xl", col, row), P("xl", row, col), P(row, col)),
        out_specs=(P("xl", col, row), P("xl"), P(row, col)),
        check_vma=False,
    )
```

time: 899 us -> 152 us (0.17)
  blocking collectives: 636 us -> 62.6 us
  waiting for transfers between devices: 233 us -> 6.31 us
  starting transfers between devices: 0.16 us -> 52.8 us
  between operations: 15.6 us -> 0.81 us
  local copies, waits for them, and re-layouts: 3.01 us -> 13.2 us
    psum x1, blocking collectives: 636 us -> 17.7 us  [local(): squared = lax.psum(squared, ('xh', 'xl'))]
    all_gather x2 -> x0, waiting for transfers between devices: 139 us -> none  [the longest x1 78.3 us: local(): grads_full = lax.all_gather(grads, 'row', axis=0, tiled=True)]
    psum x1 -> x0, waiting for transfers between devices: 92.7 us -> none  [local(): weight_grad = lax.psum(factor * grad_block, 'dp')]
    ppermute x0 -> x9, starting transfers between devices: none -> 45.2 us  [the longest x3 21.4 us: local(): far = [lax.ppermute(grads, 'za', flip(4, k)) for k in (1, 2, 3)]]
    all_to_all x0 -> x1, blocking collectives: none -> 30.7 us  [local(): lax.all_to_all(spread, ('za', 'zb', 'core', 'y'), 0, 0)]
    all_gather x0 -> x1, blocking collectives: none -> 14.2 us  [local(): mine = lax.all_gather(jnp.stack([grads, *far]), 'zb')]
  transfers between devices with their start and end apart: 4 -> 10, of which waited for: 3 -> 3; matrix products, arithmetic and copies ran while one was open for 1% -> 4% of each run, Pallas kernels for 0% -> 4%
where the time goes in v1:
time: 152 us; the launch traced here: 150 us
  blocking collectives  62.6 us (41%)
  starting transfers between devices  52.8 us (35%)
  local copies, waits for them, and re-layouts  13.2 us (9%)
  other arithmetic  8.62 us (6%)
  waiting for transfers between devices  6.31 us (4%)
  Pallas kernels  5.87 us (4%)
    all_to_all x1, blocking collectives, local(): lax.all_to_all(spread, ('za', 'zb', 'core', 'y'), 0, 0)  30.7 us
    ppermute x3, starting transfers between devices, local(): far = [lax.ppermute(grads, 'za', flip(4, k)) for k in (1, 2, 3)]  21.4 us
    psum x1, blocking collectives, local(): squared = lax.psum(squared, ('xh', 'xl'))  17.7 us
    all_gather x1, blocking collectives, local(): mine = lax.all_gather(jnp.stack([grads, *far]), 'zb')  14.2 us
    ppermute x3, starting transfers between devices, local(): got = [lax.ppermute(p, 'y', flip(4, k)) for k, p in zip((1, 2, 3), parts)]  9.83 us
    unnamed x18, local copies, waits for them, and re-layouts  9.02 us
    all_to_all x1, starting transfers between devices, local(): lax.all_to_all(jnp.broadcast_to(hidden[None], (8, F_LOC, 128)), ('xh', 'y...  7.61 us
    ppermute x1, starting transfers between devices, local(): other = lax.ppermute(mine, 'core', flip(2, 1))  6.82 us
  transfers between devices with their start and end apart: 10, of which 3 were waited for; matrix products, arithmetic and copies ran while one was open for 4% of the time, Pallas kernels for 4%

profile of v1, /device:TPU:1, one launch (start us, length us, event | category | flops | bytes accessed | tf_op | source)
XLA Modules:
  0.0 150.2 jit_solution(12325389313257255724)
XLA Ops:
  0.6 2.3 %broadcast_in_dim.20 = bf16[8,800,128]{2,1,0:T(8,128)(2,1)} broadcast(bf16[800,128]{1,0:T(8,128)(2,1)} %bitcast.31), dimensions={1,2} | broadcast | bytes 1843200 | tf_op jit(solution)/shard_map/broadcast_in_dim | solution.py:94
  2.9 7.6 %all-to-all-start = ((bf16[8,800,128]{2,1,0:T(8,128)(2,1)}), bf16[8,800,128]{2,1,0:T(8,128)(2,1)S(1)}, u32[]{:S(2)}, u32[]{:S(2)}) async-start(bf16[8,800,128]{2,1,0:T(8,128)(2,1)} %broadcast_in_dim.20), calls=%async_computation | async-start | bytes 3276800 | tf_op jit(solution)/shard_map/all_to_all | solution.py:93
  10.6 15.4 %collective-permute-start.1 = (bf16[32,640]{1,0:T(8,128)(2,1)S(1)}, bf16[32,640]{1,0:T(8,128)(2,1)S(1)}, u32[]{:S(2)}, u32[]{:S(2)}) collective-permute-start(bf16[32,640]{1,0:T(8,128)(2,1)S(1)} %bitcast.32), channel_id=1, source_target_pairs={{0,256},{128,384},{256,0},{384,128},{1,257},{129,385},{257,1},{385... | collective-permute-start | bytes 122888 | tf_op jit(solution)/shard_map/ppermute | solution.py:98
  26.0 1.9 %collective-permute-start.2 = (bf16[32,640]{1,0:T(8,128)(2,1)S(1)}, bf16[32,640]{1,0:T(8,128)(2,1)S(1)}, u32[]{:S(2)}, u32[]{:S(2)}) collective-permute-start(bf16[32,640]{1,0:T(8,128)(2,1)S(1)} %bitcast.33), channel_id=1, source_target_pairs={{0,384},{128,256},{256,128},{384,0},{1,385},{129,257},{257,129},{3... | collective-permute-start | bytes 122888 | tf_op jit(solution)/shard_map/ppermute | solution.py:98
  27.9 4.0 %collective-permute-start = (bf16[32,640]{1,0:T(8,128)(2,1)S(1)}, bf16[32,640]{1,0:T(8,128)(2,1)S(1)}, u32[]{:S(2)}, u32[]{:S(2)}) collective-permute-start(bf16[32,640]{1,0:T(8,128)(2,1)S(1)} %bitcast.34), channel_id=1, source_target_pairs={{0,128},{128,0},{256,384},{384,256},{1,129},{129,1},{257,385},{385... | collective-permute-start | bytes 122888 | tf_op jit(solution)/shard_map/ppermute | solution.py:98
  32.0 3.2 %collective-permute-done.2 = bf16[32,640]{1,0:T(8,128)(2,1)S(1)} collective-permute-done((bf16[32,640]{1,0:T(8,128)(2,1)S(1)}, bf16[32,640]{1,0:T(8,128)(2,1)S(1)}, u32[]{:S(2)}, u32[]{:S(2)}) %collective-permute-start.2) | collective-permute-done | bytes 40992 | tf_op jit(solution)/shard_map/ppermute | solution.py:98
  35.2 1.4 collective-permute-done
  36.7 14.2 %all-gather = bf16[16,32,640]{2,1,0:T(8,128)(2,1)S(1)} all-gather(bf16[4,32,640]{2,1,0:T(8,128)(2,1)S(1)} %pad_maximum_fusion), channel_id=2, replica_groups=mesh['za'=4,'zb'=4,'core'=2,'xh'=2,'y'=4,'xl'=2] {'zb'}, dimensions={0}, use_global_device_ids=true | all-gather | bytes 819200 | tf_op jit(solution)/shard_map/all_gather | solution.py:99
  50.8 6.8 %collective-permute-start.3 = (bf16[4,4,32,640]{3,2,1,0:T(8,128)(2,1)S(1)}, bf16[4,4,32,640]{3,2,1,0:T(8,128)(2,1)S(1)}, u32[]{:S(2)}, u32[]{:S(2)}) collective-permute-start(bf16[4,4,32,640]{3,2,1,0:T(8,128)(2,1)S(1)} %bitcast.29), channel_id=1, source_target_pairs={{0,16},{16,0},{1,17},{17,1},{2,18},{18,2},{3,19},{19,3},{4,20},{20... | collective-permute-start | bytes 1966088 | tf_op jit(solution)/shard_map/ppermute | solution.py:100
  57.8 1.6 %collective-permute-done.3.other = bf16[4,4,32,640]{3,2,1,0:T(8,128)(2,1)S(1)} collective-permute-done((bf16[4,4,32,640]{3,2,1,0:T(8,128)(2,1)S(1)}, bf16[4,4,32,640]{3,2,1,0:T(8,128)(2,1)S(1)}, u32[]{:S(2)}, u32[]{:S(2)}) %collective-permute-start.3) | collective-permute-done | bytes 655392 | tf_op jit(solution)/shard_map/ppermute | solution.py:100
  59.4 0.8 copy-done.3
  60.2 1.2 copy-done.2
  61.4 1.1 copy-done.4
  62.5 4.0 %input_grad_partials.1 = (bf16[1024,640]{1,0:T(8,128)(2,1)S(1)}, f32[2,800,128]{2,1,0:T(8,128)S(1)}, f32[2,800,128]{2,1,0:T(8,128)}, f32[2,800,128]{2,1,0:T(8,128)}, f32[2,800,128]{2,1,0:T(8,128)}) custom-call(s32[6]{0:T(128)S(1)} %stack.39.pos, bf16[4,4,32,640]{3,2,1,0:T(8,128)(2,1)S(1)} %bitcast.30, bf16[4,4,32,640]{3,2,1,0:T(8,128)(2,1)S(1)} %copy-done.4, ...), custom_call_target="tpu_custom_call" | custom-call | flops 1048576000 | bytes 6000000 | tf_op jit(solution)/shard_map/input_grad_partials/pallas_call | solution.py:51
  66.5 1.1 copy-done.5
  67.6 3.6 %collective-permute-start.4 = (f32[2,800,128]{2,1,0:T(8,128)}, f32[2,800,128]{2,1,0:T(8,128)}, u32[]{:S(2)}, u32[]{:S(2)}) collective-permute-start(f32[2,800,128]{2,1,0:T(8,128)} %get-tuple-element.18), channel_id=1, source_target_pairs={{0,2},{2,0},{4,6},{6,4},{1,3},{3,1},{5,7},{7,5},{8,10},{10,8},{12,... | collective-permute-start | bytes 2457608 | tf_op jit(solution)/shard_map/ppermute | solution.py:103
  71.2 4.3 %collective-permute-start.5 = (f32[2,800,128]{2,1,0:T(8,128)}, f32[2,800,128]{2,1,0:T(8,128)}, u32[]{:S(2)}, u32[]{:S(2)}) collective-permute-start(f32[2,800,128]{2,1,0:T(8,128)} %get-tuple-element.19), channel_id=1, source_target_pairs={{0,4},{2,6},{4,0},{6,2},{1,5},{3,7},{5,1},{7,3},{8,12},{10,14},{12... | collective-permute-start | bytes 2457608 | tf_op jit(solution)/shard_map/ppermute | solution.py:103
  75.5 1.9 %collective-permute-start.6 = (f32[2,800,128]{2,1,0:T(8,128)}, f32[2,800,128]{2,1,0:T(8,128)}, u32[]{:S(2)}, u32[]{:S(2)}) collective-permute-start(f32[2,800,128]{2,1,0:T(8,128)} %get-tuple-element.20), channel_id=1, source_target_pairs={{0,6},{2,4},{4,2},{6,0},{1,7},{3,5},{5,3},{7,1},{8,14},{10,12},{12... | collective-permute-start | bytes 2457608 | tf_op jit(solution)/shard_map/ppermute | solution.py:103
  77.5 1.2 copy-done
  78.6 1.4 copy-done.1
  80.1 1.3 copy-done.6
  81.4 1.9 %weight_grad_block.1 = (f32[800,640]{1,0:T(8,128)S(1)}, f32[8,128]{1,0:T(8,128)S(1)}) custom-call(bf16[8,800,128]{2,1,0:T(8,128)(2,1)S(1)} %copy-done.1, bf16[1024,640]{1,0:T(8,128)(2,1)S(1)} %copy-done.6), custom_call_target="tpu_custom_call" | custom-call | flops 1048576000 | bytes 5000000 | tf_op jit(solution)/shard_map/weight_grad_block/pallas_call | solution.py:72
  83.3 2.2 %collective-permute-start.8 = (f32[800,640]{1,0:T(8,128)S(1)}, f32[800,640]{1,0:T(8,128)}, u32[]{:S(2)}, u32[]{:S(2)}) collective-permute-start(f32[800,640]{1,0:T(8,128)S(1)} %get-tuple-element.28), channel_id=1, source_target_pairs={{0,1},{1,0},{2,3},{3,2},{4,5},{5,4},{6,7},{7,6},{8,9},{9,8},{10,11... | collective-permute-start | bytes 6144008 | tf_op jit(solution)/shard_map/ppermute | solution.py:105
  86.0 0.6 compare_select_fusion
  86.7 30.7 %all_to_all.11 = f32[128,1,2]{2,1,0:T(1,128)S(1)} all-to-all(f32[128,1,2]{2,1,0:T(1,128)S(1)} %broadcast_in_dim.23), channel_id=1, replica_groups=mesh['za'=4,'zb'=4,'core'=2,'xh'=2,'y'=4,'xl'=2] {'za','zb','core','y'}, dimensions={0} | all-to-all | bytes 2048 | tf_op jit(solution)/shard_map/all_to_all | solution.py:109
  117.6 1.8 %add_add_fusion = f32[2,800,128]{2,1,0:T(8,128)S(1)} fusion(f32[2,800,128]{2,1,0:T(8,128)} %collective-permute-done.6, f32[2,800,128]{2,1,0:T(8,128)} %collective-permute-done.5, f32[2,800,128]{2,1,0:T(8,128)S(1)} %get-tuple-element.22, f32[2,800,128]{2,1,0:T(8,128)} %collective-permute-done.4), kind=kLoop, calls=%fused_computation.1 | loop fusion | flops 614400 | bytes 4096000 | tf_op jit(solution)/shard_map/add | solution.py:111
  119.4 0.9 copy-done.7
  120.3 4.9 %collective-permute-start.7 = (f32[800,128]{1,0:T(8,128)S(1)}, f32[800,128]{1,0:T(8,128)S(1)}, u32[]{:S(2)}, u32[]{:S(2)}) collective-permute-start(f32[800,128]{1,0:T(8,128)S(1)} %slice_bitcast_fusion), channel_id=1, source_target_pairs={{0,8},{8,0},{1,9},{9,1},{2,10},{10,2},{3,11},{11,3},{4,12},{12,4},... | collective-permute-start | bytes 1228808 | tf_op jit(solution)/shard_map/ppermute | solution.py:112
  125.3 17.7 %psum.7 = f32[2]{0:T(128)S(1)} all-reduce(f32[2]{0:T(128)S(1)} %reduce_sum.9), channel_id=1, replica_groups=mesh['za'=4,'zb'=4,'core'=2,'xh'=2,'y'=4,'xl'=2] {'xh','xl'}, use_global_device_ids=true, to_apply=%region_1.2 | all-reduce | flops 2 | bytes 16 | tf_op jit(solution)/shard_map/psum | solution.py:114
  143.6 0.6 fusion.2
  144.2 1.7 %fusion.1 = bf16[1,128,800]{1,2,0:T(8,128)(2,1)} fusion(f32[800,128]{1,0:T(8,128)S(1)} %collective-permute-done.7, f32[2,800,128]{2,1,0:T(8,128)} %copy-done.7), kind=kLoop, calls=%fused_computation.5 | loop fusion | flops 204800 | bytes 1024000 | tf_op jit(solution)/shard_map/broadcast_in_dim | solution.py:120
  145.9 4.3 %multiply_add_fusion = f32[800,640]{1,0:T(8,128)} fusion(f32[800,640]{1,0:T(8,128)} %collective-permute-done.8, f32[800,640]{1,0:T(8,128)S(1)} %get-tuple-element.28, f32[]{:T(128)} %bitcast.19, f32[]{:T(128)} %bitcast.18), kind=kLoop, calls=%fused_computation | loop fusion | flops 1536000 | bytes 6144008 | tf_op jit(solution)/shard_map/add | solution.py:118
  (25 shorter events, 1.5 us)
Async XLA Ops:
  2.9 7.6 %copy-start.8 = (bf16[1,32,640]{2,1,0:T(8,128)(2,1)S(1)}, bf16[1,32,640]{2,1,0:T(8,128)(2,1)}, u32[]{:S(2)}) copy-start(bf16[1,32,640]{2,1,0:T(8,128)(2,1)} %param.4) | copy-start | bytes 122884
  2.9 74.5 %all-to-all-start = ((bf16[8,800,128]{2,1,0:T(8,128)(2,1)}), bf16[8,800,128]{2,1,0:T(8,128)(2,1)S(1)}, u32[]{:S(2)}, u32[]{:S(2)}) async-start(bf16[8,800,128]{2,1,0:T(8,128)(2,1)} %broadcast_in_dim.20), calls=%async_computation | async-start | bytes 3276800 | tf_op jit(solution)/shard_map/all_to_all | solution.py:93
  10.6 21.4 %collective-permute-start.1 = (bf16[32,640]{1,0:T(8,128)(2,1)S(1)}, bf16[32,640]{1,0:T(8,128)(2,1)S(1)}, u32[]{:S(2)}, u32[]{:S(2)}) collective-permute-start(bf16[32,640]{1,0:T(8,128)(2,1)S(1)} %bitcast.32), channel_id=1, source_target_pairs={{0,256},{128,384},{256,0},{384,128},{1,257},{129,385},{257,1},{385... | collective-permute-start | bytes 122888 | tf_op jit(solution)/shard_map/ppermute | solution.py:98
  26.0 9.2 %collective-permute-start.2 = (bf16[32,640]{1,0:T(8,128)(2,1)S(1)}, bf16[32,640]{1,0:T(8,128)(2,1)S(1)}, u32[]{:S(2)}, u32[]{:S(2)}) collective-permute-start(bf16[32,640]{1,0:T(8,128)(2,1)S(1)} %bitcast.33), channel_id=1, source_target_pairs={{0,384},{128,256},{256,128},{384,0},{1,385},{129,257},{257,129},{3... | collective-permute-start | bytes 122888 | tf_op jit(solution)/shard_map/ppermute | solution.py:98
  27.9 8.7 %collective-permute-start = (bf16[32,640]{1,0:T(8,128)(2,1)S(1)}, bf16[32,640]{1,0:T(8,128)(2,1)S(1)}, u32[]{:S(2)}, u32[]{:S(2)}) collective-permute-start(bf16[32,640]{1,0:T(8,128)(2,1)S(1)} %bitcast.34), channel_id=1, source_target_pairs={{0,128},{128,0},{256,384},{384,256},{1,129},{129,1},{257,385},{385... | collective-permute-start | bytes 122888 | tf_op jit(solution)/shard_map/ppermute | solution.py:98
  50.8 8.5 %collective-permute-start.3 = (bf16[4,4,32,640]{3,2,1,0:T(8,128)(2,1)S(1)}, bf16[4,4,32,640]{3,2,1,0:T(8,128)(2,1)S(1)}, u32[]{:S(2)}, u32[]{:S(2)}) collective-permute-start(bf16[4,4,32,640]{3,2,1,0:T(8,128)(2,1)S(1)} %bitcast.29), channel_id=1, source_target_pairs={{0,16},{16,0},{1,17},{17,1},{2,18},{18,2},{3,19},{19,3},{4,20},{20... | collective-permute-start | bytes 1966088 | tf_op jit(solution)/shard_map/ppermute | solution.py:100
  59.4 0.8 copy-start.3
  60.2 1.2 copy-start.2
  61.4 1.1 copy-start.4
  66.5 1.1 copy-start.5
  67.6 50.0 %collective-permute-start.4 = (f32[2,800,128]{2,1,0:T(8,128)}, f32[2,800,128]{2,1,0:T(8,128)}, u32[]{:S(2)}, u32[]{:S(2)}) collective-permute-start(f32[2,800,128]{2,1,0:T(8,128)} %get-tuple-element.18), channel_id=1, source_target_pairs={{0,2},{2,0},{4,6},{6,4},{1,3},{3,1},{5,7},{7,5},{8,10},{10,8},{12,... | collective-permute-start | bytes 2457608 | tf_op jit(solution)/shard_map/ppermute | solution.py:103
  71.2 46.4 %collective-permute-start.5 = (f32[2,800,128]{2,1,0:T(8,128)}, f32[2,800,128]{2,1,0:T(8,128)}, u32[]{:S(2)}, u32[]{:S(2)}) collective-permute-start(f32[2,800,128]{2,1,0:T(8,128)} %get-tuple-element.19), channel_id=1, source_target_pairs={{0,4},{2,6},{4,0},{6,2},{1,5},{3,7},{5,1},{7,3},{8,12},{10,14},{12... | collective-permute-start | bytes 2457608 | tf_op jit(solution)/shard_map/ppermute | solution.py:103
  75.5 42.1 %collective-permute-start.6 = (f32[2,800,128]{2,1,0:T(8,128)}, f32[2,800,128]{2,1,0:T(8,128)}, u32[]{:S(2)}, u32[]{:S(2)}) collective-permute-start(f32[2,800,128]{2,1,0:T(8,128)} %get-tuple-element.20), channel_id=1, source_target_pairs={{0,6},{2,4},{4,2},{6,0},{1,7},{3,5},{5,3},{7,1},{8,14},{10,12},{12... | collective-permute-start | bytes 2457608 | tf_op jit(solution)/shard_map/ppermute | solution.py:103
  77.5 1.2 copy-start
  78.6 1.4 copy-start.1
  80.1 1.3 copy-start.6
  83.3 62.7 %collective-permute-start.8 = (f32[800,640]{1,0:T(8,128)S(1)}, f32[800,640]{1,0:T(8,128)}, u32[]{:S(2)}, u32[]{:S(2)}) collective-permute-start(f32[800,640]{1,0:T(8,128)S(1)} %get-tuple-element.28), channel_id=1, source_target_pairs={{0,1},{1,0},{2,3},{3,2},{4,5},{5,4},{6,7},{7,6},{8,9},{9,8},{10,11... | collective-permute-start | bytes 6144008 | tf_op jit(solution)/shard_map/ppermute | solution.py:105
  119.4 0.9 copy-start.7
  120.3 23.9 %collective-permute-start.7 = (f32[800,128]{1,0:T(8,128)S(1)}, f32[800,128]{1,0:T(8,128)S(1)}, u32[]{:S(2)}, u32[]{:S(2)}) collective-permute-start(f32[800,128]{1,0:T(8,128)S(1)} %slice_bitcast_fusion), channel_id=1, source_target_pairs={{0,8},{8,0},{1,9},{9,1},{2,10},{10,2},{3,11},{11,3},{4,12},{12,4},... | collective-permute-start | bytes 1228808 | tf_op jit(solution)/shard_map/ppermute | solution.py:112

commit v2 on v0

v2 whole, which is shorter than its diff:
```python
import math

import jax
import jax.numpy as jnp
from jax import lax
from jax.experimental import pallas as pl
from jax.experimental.pallas import tpu as pltpu
from jax.sharding import Mesh
from jax.sharding import PartitionSpec as P

FF = 25600
D = 5120
TOK = 1024

AXES = ("za", "zb", "core", "xh", "y", "xl")
SIZES = (4, 4, 2, 2, 4, 2)
F_LOC = 800
D_LOC = 640
BF16 = jnp.bfloat16
F32 = jnp.float32
VMEM_LIMIT = 20 * 1024 * 1024

VMEM = pl.BlockSpec(memory_space=pltpu.VMEM)
SMEM = pl.BlockSpec(memory_space=pltpu.SMEM)
HBM = pl.BlockSpec(memory_space=pltpu.HBM)
PARAMS = pltpu.CompilerParams(vmem_limit_bytes=VMEM_LIMIT)


def flip(size, k):
    return [(i, i ^ k) for i in range(size)]


def fetch(pairs, sems):
    copies = [
        pltpu.make_async_copy(src, dst, sems.at[i]) for i, (src, dst) in enumerate(pairs)
    ]
    for copy in copies:
        copy.start()
    return copies


def block_grad(pos, hidden, mine, other):
    def body(pos, hidden, mine, other, out, square, full):
        xl, core = pos[5], pos[2]
        for b in range(4):
            for a in range(4):
                start = (a * 4 + b) * 64
                here, there = mine[b, a], other[b, a]
                full[start : start + 32, :] = jnp.where(core == 0, here, there)
                full[start + 32 : start + 64, :] = jnp.where(core == 0, there, here)
        lhs = jnp.concatenate([hidden[j] for j in range(8)], axis=1)
        acc = jnp.dot(lhs, full[...], preferred_element_type=F32)
        out[...] = acc
        total = jnp.sum(acc * acc)
        square[0] = jnp.where(xl == 0, total, 0.0)
        square[1] = jnp.where(xl == 1, total, 0.0)

    return pl.pallas_call(
        body,
        out_shape=(
            jax.ShapeDtypeStruct((F_LOC, D_LOC), F32),
            jax.ShapeDtypeStruct((2,), F32),
        ),
        in_specs=[SMEM, VMEM, VMEM, VMEM],
        out_specs=(VMEM, SMEM),
        scratch_shapes=[pltpu.VMEM((TOK, D_LOC), BF16)],
        compiler_params=PARAMS,
        cost_estimate=pl.CostEstimate(
            flops=2 * TOK * F_LOC * D_LOC, bytes_accessed=5_000_000, transcendentals=0
        ),
        name="own_weight_grad",
    )(pos, hidden, mine, other)


def input_parts(pos, mine, other, far, far_other, weight, far_weight):
    def body(pos, mine, other, far, far_other, w, far_w, p0, p1, p2, p3, near_t, far_t):
        core, xh, y = pos[2], pos[3], pos[4]
        for block in range(4):
            for i in range(2):
                zb, za = 2 * (block % 2) + i, block // 2
                start = (block ^ y) * 128 + i * 64
                here = pl.multiple_of(start + core * 32, 32)
                there = pl.multiple_of(start + (1 - core) * 32, 32)
                near_t[pl.ds(here, 32), :] = mine[zb, 2 * xh + za]
                near_t[pl.ds(there, 32), :] = other[zb, 2 * xh + za]
                far_t[pl.ds(here, 32), :] = far[zb, za]
                far_t[pl.ds(there, 32), :] = far_other[zb, za]
        dims = (((1,), (1,)), ((), ()))
        acc = lax.dot_general(w[...], near_t[...], dims, preferred_element_type=F32)
        acc += lax.dot_general(far_w[...], far_t[...], dims, preferred_element_type=F32)
        for k, out in enumerate((p0, p1, p2, p3)):
            out[...] = acc[:, k * 128 : (k + 1) * 128]

    part = jax.ShapeDtypeStruct((F_LOC, 128), F32)
    return pl.pallas_call(
        body,
        out_shape=(part,) * 4,
        in_specs=[SMEM] + [VMEM] * 6,
        out_specs=(VMEM,) * 4,
        scratch_shapes=[
            pltpu.VMEM((512, D_LOC), BF16),
            pltpu.VMEM((512, D_LOC), BF16),
        ],
        compiler_params=PARAMS,
        cost_estimate=pl.CostEstimate(
            flops=2 * TOK * F_LOC * D_LOC, bytes_accessed=6_000_000, transcendentals=0
        ),
        name="input_grad_partials",
    )(pos, mine, other, far, far_other, weight, far_weight)


CHUNKS = 5
ROWS = F_LOC // CHUNKS


def combine(pos, squared, block, peer):
    bound = math.sqrt(TOK * FF * D)

    def body(pos, squared, block, peer, out, b_buf, p_buf, o_buf, sems, out_sems):
        parts = [pl.ds(i * ROWS, ROWS) for i in range(CHUNKS)]
        copies = fetch(
            [(src.at[p], buf.at[p]) for p in parts for src, buf in ((block, b_buf), (peer, p_buf))],
            sems,
        )
        xl = pos[5]
        values = [jnp.full((1, D_LOC), squared[i], F32) for i in range(2)]
        factors = [1.0 / jnp.maximum(1.0, jnp.sqrt(v) / bound) for v in values]
        own = jnp.where(xl == 0, factors[0], factors[1])
        next_ = jnp.where(xl == 0, factors[1], factors[0])
        stores = []
        for i, p in enumerate(parts):
            copies[2 * i].wait()
            copies[2 * i + 1].wait()
            o_buf[p] = own * b_buf[p] + next_ * p_buf[p]
            store = pltpu.make_async_copy(o_buf.at[p], out.at[p], out_sems.at[i])
            store.start()
            stores.append(store)
        for store in stores:
            store.wait()

    buf = pltpu.VMEM((F_LOC, D_LOC), F32)
    return pl.pallas_call(
        body,
        out_shape=jax.ShapeDtypeStruct((F_LOC, D_LOC), F32),
        in_specs=[SMEM, SMEM, HBM, HBM],
        out_specs=HBM,
        scratch_shapes=[
            buf,
            buf,
            buf,
            pltpu.SemaphoreType.DMA((2 * CHUNKS,)),
            pltpu.SemaphoreType.DMA((CHUNKS,)),
        ],
        compiler_params=PARAMS,
        cost_estimate=pl.CostEstimate(
            flops=3 * F_LOC * D_LOC, bytes_accessed=6_000_000, transcendentals=0
        ),
        name="combine",
    )(pos, squared, block, peer)


def local(activations, out_grads, weight):
    pos = jnp.stack([lax.axis_index(a) for a in AXES]).astype(jnp.int32)
    xh, xl = pos[3], pos[5]

    hidden = lax.all_to_all(
        jnp.broadcast_to(activations[0].T[None], (8, F_LOC, 128)), ("xh", "y"), 0, 0
    )
    far_weight = lax.ppermute(weight, ("xh", "xl"), [(i, 3 - i) for i in range(4)])

    mine = lax.all_gather(lax.all_gather(out_grads[0], "za"), "zb")
    other = lax.ppermute(mine, "core", flip(2, 1))
    away = lax.dynamic_slice_in_dim(mine, 2 * (1 - xh), 2, axis=1)
    far = lax.ppermute(away, "xh", flip(2, 1))

    other, far_weight = lax.optimization_barrier((other, far_weight))
    block, squared = block_grad(pos, hidden, mine, other)
    squared = lax.psum(squared, ("xh", "xl"))
    far, squared, block = lax.optimization_barrier((far, squared, block))
    next_block = lax.ppermute(block, "xl", flip(2, 1))
    far_other = lax.ppermute(far, "core", flip(2, 1))
    p0, *parts = input_parts(pos, mine, other, far, far_other, weight, far_weight)
    squared, p0 = lax.optimization_barrier((squared, p0))
    got = [lax.ppermute(p, "y", flip(4, k)) for k, p in zip((1, 2, 3), parts)]
    input_grads = (p0 + got[0] + got[1] + got[2]).astype(BF16).T[None]

    spread = jnp.broadcast_to(squared, (128, 2))
    squared = jnp.sum(lax.all_to_all(spread, ("za", "zb", "core", "y"), 0, 0), axis=0)
    norms = jnp.sqrt(squared)
    weight_grad = combine(pos, squared, block, next_block)
    return (input_grads, jnp.reshape(norms[xl], (1,)), weight_grad)


def solution(mesh):
    fine = Mesh(mesh.devices.reshape(SIZES), AXES)
    row, col = ("za", "zb", "core"), ("xh", "y")
    return jax.shard_map(
        local,
        mesh=fine,
        in_specs=(P("xl", col, row), P("xl", row, col), P(row, col)),
        out_specs=(P("xl", col, row), P("xl"), P(row, col)),
        check_vma=False,
    )
```

time: 899 us -> 135 us (0.15)
  blocking collectives: 636 us -> 46.5 us
  waiting for transfers between devices: 233 us -> 17.1 us
  starting transfers between devices: 0.16 us -> 48.2 us
  between operations: 15.6 us -> 0.77 us
  Pallas kernels: 0 us -> 11.3 us
    psum x1, blocking collectives: 636 us -> 8.81 us  [local(): squared = lax.psum(squared, ('xh', 'xl'))]
    all_gather x2 -> x0, waiting for transfers between devices: 139 us -> none  [the longest x1 78.3 us: local(): grads_full = lax.all_gather(grads, 'row', axis=0, tiled=True)]
    psum x1 -> x0, waiting for transfers between devices: 92.7 us -> none  [local(): weight_grad = lax.psum(factor * grad_block, 'dp')]
    all_gather x0 -> x2, blocking collectives: none -> 37.6 us  [local(): mine = lax.all_gather(lax.all_gather(out_grads[0], 'za'), 'zb')]
    ppermute x0 -> x8, starting transfers between devices: none -> 30 us  [the longest x3 9.57 us: local(): got = [lax.ppermute(p, 'y', flip(4, k)) for k, p in zip((1, 2, 3), parts)]]
    all_to_all x0 -> x2, starting transfers between devices: none -> 18.2 us  [the longest x1 10.6 us: local(): lax.all_to_all(spread, ('za', 'zb', 'core', 'y'), 0, 0)]
    all_to_all x0 -> x2, waiting for transfers between devices: none -> 15.7 us  [the longest x1 15.7 us: local(): lax.all_to_all(spread, ('za', 'zb', 'core', 'y'), 0, 0)]
    pallas_call x0 -> x3, Pallas kernels: none -> 11.3 us  [the longest x1 4.08 us: input_parts(): pl.pallas_call(body, out_shape=(part,) * 4, in_specs=[SMEM] + [VMEM] * 6,...]
  transfers between devices with their start and end apart: 4 -> 10, of which waited for: 3 -> 2; matrix products, arithmetic and copies ran while one was open for 1% -> 3% of each run, Pallas kernels for 0% -> 6%
where the time goes in v2:
time: 135 us; the launch traced here: 134 us
  starting transfers between devices  48.2 us (36%)
  blocking collectives  46.5 us (34%)
  waiting for transfers between devices  17.1 us (13%)
  Pallas kernels  11.3 us (8%)
  local copies, waits for them, and re-layouts  8.22 us (6%)
  other arithmetic  2.03 us (2%)
    all_gather x2, blocking collectives, local(): mine = lax.all_gather(lax.all_gather(out_grads[0], 'za'), 'zb')  37.6 us
    all_to_all x1, waiting for transfers between devices, local(): lax.all_to_all(spread, ('za', 'zb', 'core', 'y'), 0, 0)  15.7 us
    all_to_all x1, starting transfers between devices, local(): lax.all_to_all(spread, ('za', 'zb', 'core', 'y'), 0, 0)  10.6 us
    ppermute x3, starting transfers between devices, local(): got = [lax.ppermute(p, 'y', flip(4, k)) for k, p in zip((1, 2, 3), parts)]  9.57 us
    psum x1, blocking collectives, local(): squared = lax.psum(squared, ('xh', 'xl'))  8.81 us
    ppermute x1, starting transfers between devices, local(): other = lax.ppermute(mine, 'core', flip(2, 1))  7.66 us
    all_to_all x1, starting transfers between devices, local(): lax.all_to_all(jnp.broadcast_to(activations[0].T[None], (8, F_LOC, 128)),...  7.61 us
    ppermute x1, starting transfers between devices, local(): lax.ppermute(weight, ('xh', 'xl'), [(i, 3 - i) for i in range(4)])  4.6 us
  transfers between devices with their start and end apart: 10, of which 2 were waited for; matrix products, arithmetic and copies ran while one was open for 3% of the time, Pallas kernels for 6%

profile of v2, /device:TPU:1, one launch (start us, length us, event | category | flops | bytes accessed | tf_op | source)
XLA Modules:
  0.0 134.2 jit_solution(15635399102726554332)
XLA Ops:
  0.6 2.3 %broadcast_in_dim.12 = bf16[8,800,128]{2,1,0:T(8,128)(2,1)} broadcast(bf16[800,128]{1,0:T(8,128)(2,1)} %bitcast.18), dimensions={1,2} | broadcast | bytes 1843200 | tf_op jit(solution)/shard_map/broadcast_in_dim | solution.py:167
  2.9 7.6 %all-to-all-start = ((bf16[8,800,128]{2,1,0:T(8,128)(2,1)}), bf16[8,800,128]{2,1,0:T(8,128)(2,1)S(1)}, u32[]{:S(2)}, u32[]{:S(2)}) async-start(bf16[8,800,128]{2,1,0:T(8,128)(2,1)} %broadcast_in_dim.12), calls=%async_computation | async-start | bytes 3276800 | tf_op jit(solution)/shard_map/all_to_all | solution.py:166
  10.6 4.6 %collective-permute-start.2 = (bf16[800,640]{1,0:T(8,128)(2,1)S(1)}, bf16[800,640]{1,0:T(8,128)(2,1)}, u32[]{:S(2)}, u32[]{:S(2)}) collective-permute-start(bf16[800,640]{1,0:T(8,128)(2,1)S(1)} %copy-done.2), channel_id=1, source_target_pairs={{0,9},{1,8},{8,1},{9,0},{2,11},{3,10},{10,3},{11,2},{4,13},{5,12},... | collective-permute-start | bytes 3072008 | tf_op jit(solution)/shard_map/ppermute | solution.py:169
  15.2 24.0 %all_gather.9 = bf16[4,32,640]{2,1,0:T(8,128)(2,1)S(1)} all-gather(bf16[1,32,640]{2,1,0:T(8,128)(2,1)S(1)} %copy-done.4), channel_id=1, replica_groups=mesh['za'=4,'zb'=4,'core'=2,'xh'=2,'y'=4,'xl'=2] {'za'}, dimensions={0}, use_global_device_ids=true | all-gather | bytes 204800 | tf_op jit(solution)/shard_map/all_gather | solution.py:171
  39.2 13.7 %all-gather = bf16[16,32,640]{2,1,0:T(8,128)(2,1)S(1)} all-gather(bf16[4,32,640]{2,1,0:T(8,128)(2,1)S(1)} %all_gather.9), channel_id=2, replica_groups=mesh['za'=4,'zb'=4,'core'=2,'xh'=2,'y'=4,'xl'=2] {'zb'}, dimensions={0}, use_global_device_ids=true | all-gather | bytes 819200 | tf_op jit(solution)/shard_map/all_gather | solution.py:171
  52.8 7.7 %collective-permute-start.1 = (bf16[4,4,32,640]{3,2,1,0:T(8,128)(2,1)S(1)}, bf16[4,4,32,640]{3,2,1,0:T(8,128)(2,1)}, u32[]{:S(2)}, u32[]{:S(2)}) collective-permute-start(bf16[4,4,32,640]{3,2,1,0:T(8,128)(2,1)S(1)} %bitcast.14), channel_id=1, source_target_pairs={{0,16},{16,0},{1,17},{17,1},{2,18},{18,2},{3,19},{19,3},{4,20},{20... | collective-permute-start | bytes 1966088 | tf_op jit(solution)/shard_map/ppermute | solution.py:172
  60.5 0.8 constant_dynamic-slice_fusion
  61.2 2.0 %collective-permute-start = (bf16[4,2,32,640]{3,2,1,0:T(8,128)(2,1)}, bf16[4,2,32,640]{3,2,1,0:T(8,128)(2,1)}, u32[]{:S(2)}, u32[]{:S(2)}) collective-permute-start(bf16[4,2,32,640]{3,2,1,0:T(8,128)(2,1)} %constant_dynamic-slice_fusion), channel_id=1, source_target_pairs={{0,8},{8,0},{1,9},{9,1},{2,10},{10,2},{3,11},{11,3},{4,12},{12,4},... | collective-permute-start | bytes 983048 | tf_op jit(solution)/shard_map/ppermute | solution.py:174
  63.3 0.1 stack.27.pos
  63.4 0.0 collective-permute-done.2.far_w
  63.4 0.0 copy-start
  63.4 1.2 copy-done
  64.6 1.4 %copy-done.1 = bf16[8,800,128]{2,1,0:T(8,128)(2,1)S(1)} copy-done((bf16[8,800,128]{2,1,0:T(8,128)(2,1)S(1)}, bf16[8,800,128]{2,1,0:T(8,128)(2,1)}, u32[]{:S(2)}) %copy-start.1) | copy-done | bytes 1638424
  66.0 3.6 %own_weight_grad.1 = (f32[800,640]{1,0:T(8,128)S(1)}, f32[2]{0:T(128)S(1)}) custom-call(s32[6]{0:T(128)S(1)} %stack.27.pos, bf16[8,800,128]{2,1,0:T(8,128)(2,1)S(1)} %copy-done.1, bf16[4,4,32,640]{3,2,1,0:T(8,128)(2,1)S(1)} %bitcast.16, bf16[4,4,32,640]{3,2,1,0:T(8,128)(2,1)} %collective-permute-done.1.other), custom_call_target="tpu_custom_call" | custom-call | flops 1048576000 | bytes 5000000 | tf_op jit(solution)/shard_map/own_weight_grad/pallas_call | solution.py:58
  69.6 8.8 %psum.7 = f32[2]{0:T(128)S(1)} all-reduce(f32[2]{0:T(128)S(1)} %get-tuple-element.17), channel_id=1, replica_groups=mesh['za'=4,'zb'=4,'core'=2,'xh'=2,'y'=4,'xl'=2] {'xh','xl'}, use_global_device_ids=true, to_apply=%region_0.0 | all-reduce | flops 2 | bytes 16 | tf_op jit(solution)/shard_map/psum | solution.py:178
  78.4 1.9 %collective-permute-start.7 = (f32[800,640]{1,0:T(8,128)S(1)}, f32[800,640]{1,0:T(8,128)}, u32[]{:S(2)}, u32[]{:S(2)}) collective-permute-start(f32[800,640]{1,0:T(8,128)S(1)} %get-tuple-element.28.block), channel_id=1, source_target_pairs={{0,1},{1,0},{2,3},{3,2},{4,5},{5,4},{6,7},{7,6},{8,9},{9,8},{10,11... | collective-permute-start | bytes 6144008 | tf_op jit(solution)/shard_map/ppermute | solution.py:180
  80.3 4.2 %collective-permute-start.3 = (bf16[4,2,32,640]{3,2,1,0:T(8,128)(2,1)}, bf16[4,2,32,640]{3,2,1,0:T(8,128)(2,1)S(1)}, u32[]{:S(2)}, u32[]{:S(2)}) collective-permute-start(bf16[4,2,32,640]{3,2,1,0:T(8,128)(2,1)} %collective-permute-done.far), channel_id=1, source_target_pairs={{0,16},{16,0},{1,17},{17,1},{2,18},{18,2},{3,19},{19,3},{4,20},{20... | collective-permute-start | bytes 983048 | tf_op jit(solution)/shard_map/ppermute | solution.py:181
  84.6 1.4 %collective-permute-done.3.far_other = bf16[4,2,32,640]{3,2,1,0:T(8,128)(2,1)S(1)} collective-permute-done((bf16[4,2,32,640]{3,2,1,0:T(8,128)(2,1)}, bf16[4,2,32,640]{3,2,1,0:T(8,128)(2,1)S(1)}, u32[]{:S(2)}, u32[]{:S(2)}) %collective-permute-start.3) | collective-permute-done | bytes 327712 | tf_op jit(solution)/shard_map/ppermute | solution.py:181
  86.0 1.2 copy-done.3
  87.2 4.1 %input_grad_partials.1 = (f32[800,128]{1,0:T(8,128)S(1)}, f32[800,128]{1,0:T(8,128)}, f32[800,128]{1,0:T(8,128)}, f32[800,128]{1,0:T(8,128)}) custom-call(s32[6]{0:T(128)S(1)} %stack.27.pos, bf16[4,4,32,640]{3,2,1,0:T(8,128)(2,1)S(1)} %bitcast.17, bf16[4,4,32,640]{3,2,1,0:T(8,128)(2,1)} %collective-permute-done.1.other, ...), custom_call_target="tpu_custom_call" | custom-call | flops 1048576000 | bytes 6000000 | tf_op jit(solution)/shard_map/input_grad_partials/pallas_call | solution.py:95
  91.3 2.4 %collective-permute-start.4 = (f32[800,128]{1,0:T(8,128)}, f32[800,128]{1,0:T(8,128)S(1)}, u32[]{:S(2)}, u32[]{:S(2)}) collective-permute-start(f32[800,128]{1,0:T(8,128)} %get-tuple-element.24), channel_id=1, source_target_pairs={{0,2},{2,0},{4,6},{6,4},{1,3},{3,1},{5,7},{7,5},{8,10},{10,8},{12,... | collective-permute-start | bytes 1228808 | tf_op jit(solution)/shard_map/ppermute | solution.py:184
  93.8 4.2 %collective-permute-start.5 = (f32[800,128]{1,0:T(8,128)}, f32[800,128]{1,0:T(8,128)}, u32[]{:S(2)}, u32[]{:S(2)}) collective-permute-start(f32[800,128]{1,0:T(8,128)} %get-tuple-element.25), channel_id=1, source_target_pairs={{0,4},{2,6},{4,0},{6,2},{1,5},{3,7},{5,1},{7,3},{8,12},{10,14},{12... | collective-permute-start | bytes 1228808 | tf_op jit(solution)/shard_map/ppermute | solution.py:184
  98.0 2.9 %collective-permute-start.6 = (f32[800,128]{1,0:T(8,128)}, f32[800,128]{1,0:T(8,128)}, u32[]{:S(2)}, u32[]{:S(2)}) collective-permute-start(f32[800,128]{1,0:T(8,128)} %get-tuple-element.26), channel_id=1, source_target_pairs={{0,6},{2,4},{4,2},{6,0},{1,7},{3,5},{5,3},{7,1},{8,14},{10,12},{12... | collective-permute-start | bytes 1228808 | tf_op jit(solution)/shard_map/ppermute | solution.py:184
  100.9 0.7 broadcast_in_dim.14
  101.6 10.6 %all-to-all-start.1 = ((f32[128,1,2]{2,1,0:T(1,128)}), f32[128,1,2]{2,1,0:T(1,128)S(1)}, u32[]{:S(2)}, u32[]{:S(2)}) async-start(f32[128,1,2]{2,1,0:T(1,128)} %broadcast_in_dim.14), calls=%async_computation.1 | async-start | bytes 131072 | tf_op jit(solution)/shard_map/all_to_all | solution.py:188
  112.2 15.7 %all-to-all-done.1 = f32[128,1,2]{2,1,0:T(1,128)S(1)} async-done(((f32[128,1,2]{2,1,0:T(1,128)}), f32[128,1,2]{2,1,0:T(1,128)S(1)}, u32[]{:S(2)}, u32[]{:S(2)}) %all-to-all-start.1) | async-done | bytes 1056 | tf_op jit(solution)/shard_map/all_to_all | solution.py:188
  127.9 0.2 reduce_sum.9.squared
  128.0 0.6 dynamic_slice.7
  128.6 0.0 collective-permute-done.4
  128.6 0.0 collective-permute-done.5
  128.6 1.9 %fusion = bf16[1,128,800]{1,2,0:T(8,128)(2,1)} fusion(f32[800,128]{1,0:T(8,128)} %collective-permute-done.6, f32[800,128]{1,0:T(8,128)} %collective-permute-done.5, f32[800,128]{1,0:T(8,128)S(1)} %get-tuple-element.23, f32[800,128]{1,0:T(8,128)S(1)} %collective-permute-done.4), kind=kLoop, calls=%fused_computation.1 | loop fusion | flops 409600 | bytes 1843200 | tf_op jit(solution)/shard_map/broadcast_in_dim | solution.py:185
  130.5 3.6 %combine.1 = f32[800,640]{1,0:T(8,128)} custom-call(s32[6]{0:T(128)S(1)} %stack.27.pos, f32[2]{0:T(128)S(1)} %reduce_sum.9.squared, f32[800,640]{1,0:T(8,128)S(1)} %get-tuple-element.28.block, f32[800,640]{1,0:T(8,128)} %collective-permute-done.7.peer), custom_call_target="tpu_custom_call" | custom-call | flops 1536000 | bytes 6000000 | tf_op jit(solution)/shard_map/combine/pallas_call | solution.py:142
  (12 shorter events, 0.0 us)
Async XLA Ops:
  2.9 7.6 %copy-start.2 = (bf16[800,640]{1,0:T(8,128)(2,1)S(1)}, bf16[800,640]{1,0:T(8,128)(2,1)}, u32[]{:S(2)}) copy-start(bf16[800,640]{1,0:T(8,128)(2,1)} %w.1) | copy-start | bytes 3072004
  2.9 12.2 %copy-start.4 = (bf16[1,32,640]{2,1,0:T(8,128)(2,1)S(1)}, bf16[1,32,640]{2,1,0:T(8,128)(2,1)}, u32[]{:S(2)}) copy-start(bf16[1,32,640]{2,1,0:T(8,128)(2,1)} %param.4) | copy-start | bytes 122884
  2.9 60.4 %all-to-all-start = ((bf16[8,800,128]{2,1,0:T(8,128)(2,1)}), bf16[8,800,128]{2,1,0:T(8,128)(2,1)S(1)}, u32[]{:S(2)}, u32[]{:S(2)}) async-start(bf16[8,800,128]{2,1,0:T(8,128)(2,1)} %broadcast_in_dim.12), calls=%async_computation | async-start | bytes 3276800 | tf_op jit(solution)/shard_map/all_to_all | solution.py:166
  10.6 52.8 %collective-permute-start.2 = (bf16[800,640]{1,0:T(8,128)(2,1)S(1)}, bf16[800,640]{1,0:T(8,128)(2,1)}, u32[]{:S(2)}, u32[]{:S(2)}) collective-permute-start(bf16[800,640]{1,0:T(8,128)(2,1)S(1)} %copy-done.2), channel_id=1, source_target_pairs={{0,9},{1,8},{8,1},{9,0},{2,11},{3,10},{10,3},{11,2},{4,13},{5,12},... | collective-permute-start | bytes 3072008 | tf_op jit(solution)/shard_map/ppermute | solution.py:169
  52.8 10.6 %collective-permute-start.1 = (bf16[4,4,32,640]{3,2,1,0:T(8,128)(2,1)S(1)}, bf16[4,4,32,640]{3,2,1,0:T(8,128)(2,1)}, u32[]{:S(2)}, u32[]{:S(2)}) collective-permute-start(bf16[4,4,32,640]{3,2,1,0:T(8,128)(2,1)S(1)} %bitcast.14), channel_id=1, source_target_pairs={{0,16},{16,0},{1,17},{17,1},{2,18},{18,2},{3,19},{19,3},{4,20},{20... | collective-permute-start | bytes 1966088 | tf_op jit(solution)/shard_map/ppermute | solution.py:172
  61.2 17.2 %collective-permute-start = (bf16[4,2,32,640]{3,2,1,0:T(8,128)(2,1)}, bf16[4,2,32,640]{3,2,1,0:T(8,128)(2,1)}, u32[]{:S(2)}, u32[]{:S(2)}) collective-permute-start(bf16[4,2,32,640]{3,2,1,0:T(8,128)(2,1)} %constant_dynamic-slice_fusion), channel_id=1, source_target_pairs={{0,8},{8,0},{1,9},{9,1},{2,10},{10,2},{3,11},{11,3},{4,12},{12,4},... | collective-permute-start | bytes 983048 | tf_op jit(solution)/shard_map/ppermute | solution.py:174
  63.4 1.2 copy-start
  64.6 1.4 %copy-start.1 = (bf16[8,800,128]{2,1,0:T(8,128)(2,1)S(1)}, bf16[8,800,128]{2,1,0:T(8,128)(2,1)}, u32[]{:S(2)}) copy-start(bf16[8,800,128]{2,1,0:T(8,128)(2,1)} %copy-done) | copy-start | bytes 4915204
  78.4 52.1 %collective-permute-start.7 = (f32[800,640]{1,0:T(8,128)S(1)}, f32[800,640]{1,0:T(8,128)}, u32[]{:S(2)}, u32[]{:S(2)}) collective-permute-start(f32[800,640]{1,0:T(8,128)S(1)} %get-tuple-element.28.block), channel_id=1, source_target_pairs={{0,1},{1,0},{2,3},{3,2},{4,5},{5,4},{6,7},{7,6},{8,9},{9,8},{10,11... | collective-permute-start | bytes 6144008 | tf_op jit(solution)/shard_map/ppermute | solution.py:180
  80.3 5.7 %collective-permute-start.3 = (bf16[4,2,32,640]{3,2,1,0:T(8,128)(2,1)}, bf16[4,2,32,640]{3,2,1,0:T(8,128)(2,1)S(1)}, u32[]{:S(2)}, u32[]{:S(2)}) collective-permute-start(bf16[4,2,32,640]{3,2,1,0:T(8,128)(2,1)} %collective-permute-done.far), channel_id=1, source_target_pairs={{0,16},{16,0},{1,17},{17,1},{2,18},{18,2},{3,19},{19,3},{4,20},{20... | collective-permute-start | bytes 983048 | tf_op jit(solution)/shard_map/ppermute | solution.py:181
  86.0 1.2 copy-start.3
  91.3 37.3 %collective-permute-start.4 = (f32[800,128]{1,0:T(8,128)}, f32[800,128]{1,0:T(8,128)S(1)}, u32[]{:S(2)}, u32[]{:S(2)}) collective-permute-start(f32[800,128]{1,0:T(8,128)} %get-tuple-element.24), channel_id=1, source_target_pairs={{0,2},{2,0},{4,6},{6,4},{1,3},{3,1},{5,7},{7,5},{8,10},{10,8},{12,... | collective-permute-start | bytes 1228808 | tf_op jit(solution)/shard_map/ppermute | solution.py:184
  93.8 34.9 %collective-permute-start.5 = (f32[800,128]{1,0:T(8,128)}, f32[800,128]{1,0:T(8,128)}, u32[]{:S(2)}, u32[]{:S(2)}) collective-permute-start(f32[800,128]{1,0:T(8,128)} %get-tuple-element.25), channel_id=1, source_target_pairs={{0,4},{2,6},{4,0},{6,2},{1,5},{3,7},{5,1},{7,3},{8,12},{10,14},{12... | collective-permute-start | bytes 1228808 | tf_op jit(solution)/shard_map/ppermute | solution.py:184
  98.0 30.7 %collective-permute-start.6 = (f32[800,128]{1,0:T(8,128)}, f32[800,128]{1,0:T(8,128)}, u32[]{:S(2)}, u32[]{:S(2)}) collective-permute-start(f32[800,128]{1,0:T(8,128)} %get-tuple-element.26), channel_id=1, source_target_pairs={{0,6},{2,4},{4,2},{6,0},{1,7},{3,5},{5,3},{7,1},{8,14},{10,12},{12... | collective-permute-start | bytes 1228808 | tf_op jit(solution)/shard_map/ppermute | solution.py:184
  101.6 26.3 %all-to-all-start.1 = ((f32[128,1,2]{2,1,0:T(1,128)}), f32[128,1,2]{2,1,0:T(1,128)S(1)}, u32[]{:S(2)}, u32[]{:S(2)}) async-start(f32[128,1,2]{2,1,0:T(1,128)} %broadcast_in_dim.14), calls=%async_computation.1 | async-start | bytes 131072 | tf_op jit(solution)/shard_map/all_to_all | solution.py:188

commit v3 on v2

--- a/solution.py
+++ b/solution.py
@@ -113,26 +113,33 @@
 ROWS = F_LOC // CHUNKS
 
 
-def combine(pos, squared, block, peer):
+def combine(pos, squared, block, peer, parts):
     bound = math.sqrt(TOK * FF * D)
 
-    def body(pos, squared, block, peer, out, b_buf, p_buf, o_buf, sems, out_sems):
-        parts = [pl.ds(i * ROWS, ROWS) for i in range(CHUNKS)]
-        copies = fetch(
-            [(src.at[p], buf.at[p]) for p in parts for src, buf in ((block, b_buf), (peer, p_buf))],
-            sems,
-        )
+    def body(
+        pos, squared, block, peer, q0, q1, q2, q3, out, tokens, norm,
+        b_buf, p_buf, o_buf, q_buf, sems, out_sems,
+    ):
+        rows = [pl.ds(i * ROWS, ROWS) for i in range(CHUNKS)]
+        pairs = [(q, q_buf.at[i]) for i, q in enumerate((q0, q1, q2, q3))]
+        for r in rows:
+            pairs += [(block.at[r], b_buf.at[r]), (peer.at[r], p_buf.at[r])]
+        copies = fetch(pairs, sems)
         xl = pos[5]
-        values = [jnp.full((1, D_LOC), squared[i], F32) for i in range(2)]
-        factors = [1.0 / jnp.maximum(1.0, jnp.sqrt(v) / bound) for v in values]
+        norms = [jnp.sqrt(jnp.full((8, D_LOC), squared[i], F32)) for i in range(2)]
+        factors = [(1.0 / jnp.maximum(1.0, v / bound))[:1] for v in norms]
         own = jnp.where(xl == 0, factors[0], factors[1])
         next_ = jnp.where(xl == 0, factors[1], factors[0])
+        norm[0] = jnp.max(jnp.where(xl == 0, norms[0], norms[1]))
+        for copy in copies[:4]:
+            copy.wait()
+        tokens[...] = (q_buf[0] + q_buf[1] + q_buf[2] + q_buf[3]).astype(BF16)
         stores = []
-        for i, p in enumerate(parts):
-            copies[2 * i].wait()
-            copies[2 * i + 1].wait()
-            o_buf[p] = own * b_buf[p] + next_ * p_buf[p]
-            store = pltpu.make_async_copy(o_buf.at[p], out.at[p], out_sems.at[i])
+        for i, r in enumerate(rows):
+            copies[4 + 2 * i].wait()
+            copies[5 + 2 * i].wait()
+            o_buf[r] = own * b_buf[r] + next_ * p_buf[r]
+            store = pltpu.make_async_copy(o_buf.at[r], out.at[r], out_sems.at[i])
             store.start()
             stores.append(store)
         for store in stores:
@@ -141,27 +148,32 @@
     buf = pltpu.VMEM((F_LOC, D_LOC), F32)
     return pl.pallas_call(
         body,
-        out_shape=jax.ShapeDtypeStruct((F_LOC, D_LOC), F32),
-        in_specs=[SMEM, SMEM, HBM, HBM],
-        out_specs=HBM,
+        out_shape=(
+            jax.ShapeDtypeStruct((F_LOC, D_LOC), F32),
+            jax.ShapeDtypeStruct((F_LOC, 128), BF16),
+            jax.ShapeDtypeStruct((1,), F32),
+        ),
+        in_specs=[SMEM, SMEM] + [HBM] * 6,
+        out_specs=(HBM, VMEM, SMEM),
         scratch_shapes=[
             buf,
             buf,
             buf,
-            pltpu.SemaphoreType.DMA((2 * CHUNKS,)),
+            pltpu.VMEM((4, F_LOC, 128), F32),
+            pltpu.SemaphoreType.DMA((4 + 2 * CHUNKS,)),
             pltpu.SemaphoreType.DMA((CHUNKS,)),
         ],
         compiler_params=PARAMS,
         cost_estimate=pl.CostEstimate(
-            flops=3 * F_LOC * D_LOC, bytes_accessed=6_000_000, transcendentals=0
+            flops=3 * F_LOC * D_LOC, bytes_accessed=8_000_000, transcendentals=0
         ),
         name="combine",
-    )(pos, squared, block, peer)
+    )(pos, squared, block, peer, *parts)
 
 
 def local(activations, out_grads, weight):
     pos = jnp.stack([lax.axis_index(a) for a in AXES]).astype(jnp.int32)
-    xh, xl = pos[3], pos[5]
+    xh = pos[3]
 
     hidden = lax.all_to_all(
         jnp.broadcast_to(activations[0].T[None], (8, F_LOC, 128)), ("xh", "y"), 0, 0
@@ -182,13 +194,11 @@
     p0, *parts = input_parts(pos, mine, other, far, far_other, weight, far_weight)
     squared, p0 = lax.optimization_barrier((squared, p0))
     got = [lax.ppermute(p, "y", flip(4, k)) for k, p in zip((1, 2, 3), parts)]
-    input_grads = (p0 + got[0] + got[1] + got[2]).astype(BF16).T[None]
 
     spread = jnp.broadcast_to(squared, (128, 2))
     squared = jnp.sum(lax.all_to_all(spread, ("za", "zb", "core", "y"), 0, 0), axis=0)
-    norms = jnp.sqrt(squared)
-    weight_grad = combine(pos, squared, block, next_block)
-    return (input_grads, jnp.reshape(norms[xl], (1,)), weight_grad)
+    weight_grad, tokens, norm = combine(pos, squared, block, next_block, (p0, *got))
+    return (tokens.T[None], norm, weight_grad)
 
 
 def solution(mesh):

time: 135 us -> 133 us (0.985)
  blocking collectives: 46.5 us -> 72.6 us
  waiting for transfers between devices: 17.1 us -> 1.47 us
  starting transfers between devices: 48.2 us -> 37.6 us
  other arithmetic: 2.03 us -> 0.15 us
  Pallas kernels: 11.3 us -> 12.7 us
    all_to_all x0 -> x1, blocking collectives: none -> 26.2 us  [local(): lax.all_to_all(spread, ('za', 'zb', 'core', 'y'), 0, 0)]
    all_to_all x1 -> x0, waiting for transfers between devices: 15.7 us -> none  [local(): lax.all_to_all(spread, ('za', 'zb', 'core', 'y'), 0, 0)]
    all_to_all x1 -> x0, starting transfers between devices: 10.6 us -> none  [local(): lax.all_to_all(spread, ('za', 'zb', 'core', 'y'), 0, 0)]
    broadcast_in_dim x1 -> x0, other arithmetic: 1.88 us -> none  [local(): input_grads = (p0 + got[0] + got[1] + got[2]).astype(BF16).T[None]]
    pallas_call x1, Pallas kernels: 3.64 us -> 5 us  [combine(): pl.pallas_call(body, out_shape=(jax.ShapeDtypeStruct((F_LOC, D_LOC), F32)...]
  transfers between devices with their start and end apart: 10 -> 9, of which waited for: 2 -> 1; matrix products, arithmetic and copies ran while one was open for 3% -> 1% of each run, Pallas kernels for 6% -> 6%
where the time goes in v3:
time: 133 us; the launch traced here: 132 us
  blocking collectives  72.6 us (55%)
  starting transfers between devices  37.6 us (28%)
  Pallas kernels  12.7 us (10%)
  local copies, waits for them, and re-layouts  6.99 us (5%)
  waiting for transfers between devices  1.47 us (1%)
    all_gather x2, blocking collectives, local(): mine = lax.all_gather(lax.all_gather(out_grads[0], 'za'), 'zb')  37.6 us
    all_to_all x1, blocking collectives, local(): lax.all_to_all(spread, ('za', 'zb', 'core', 'y'), 0, 0)  26.2 us
    ppermute x3, starting transfers between devices, local(): got = [lax.ppermute(p, 'y', flip(4, k)) for k, p in zip((1, 2, 3), parts)]  9.57 us
    psum x1, blocking collectives, local(): squared = lax.psum(squared, ('xh', 'xl'))  8.81 us
    ppermute x1, starting transfers between devices, local(): other = lax.ppermute(mine, 'core', flip(2, 1))  7.66 us
    all_to_all x1, starting transfers between devices, local(): lax.all_to_all(jnp.broadcast_to(activations[0].T[None], (8, F_LOC, 128)),...  7.61 us
    pallas_call x1, Pallas kernels, combine(): pl.pallas_call(body, out_shape=(jax.ShapeDtypeStruct((F_LOC, D_LOC), F32)...  5 us
    ppermute x1, starting transfers between devices, local(): lax.ppermute(weight, ('xh', 'xl'), [(i, 3 - i) for i in range(4)])  4.6 us
  transfers between devices with their start and end apart: 9, of which 1 were waited for; matrix products, arithmetic and copies ran while one was open for 1% of the time, Pallas kernels for 6%

profile of v3, /device:TPU:1, one launch (start us, length us, event | category | flops | bytes accessed | tf_op | source)
XLA Modules:
  0.0 132.3 jit_solution(6059495625241392765)
XLA Ops:
  0.6 2.3 %broadcast_in_dim.12 = bf16[8,800,128]{2,1,0:T(8,128)(2,1)} broadcast(bf16[800,128]{1,0:T(8,128)(2,1)} %bitcast.17), dimensions={1,2} | broadcast | bytes 1843200 | tf_op jit(solution)/shard_map/broadcast_in_dim | solution.py:179
  2.9 7.6 %all-to-all-start = ((bf16[8,800,128]{2,1,0:T(8,128)(2,1)}), bf16[8,800,128]{2,1,0:T(8,128)(2,1)S(1)}, u32[]{:S(2)}, u32[]{:S(2)}) async-start(bf16[8,800,128]{2,1,0:T(8,128)(2,1)} %broadcast_in_dim.12), calls=%async_computation | async-start | bytes 3276800 | tf_op jit(solution)/shard_map/all_to_all | solution.py:178
  10.6 4.6 %collective-permute-start.2 = (bf16[800,640]{1,0:T(8,128)(2,1)S(1)}, bf16[800,640]{1,0:T(8,128)(2,1)}, u32[]{:S(2)}, u32[]{:S(2)}) collective-permute-start(bf16[800,640]{1,0:T(8,128)(2,1)S(1)} %copy-done.2), channel_id=1, source_target_pairs={{0,9},{1,8},{8,1},{9,0},{2,11},{3,10},{10,3},{11,2},{4,13},{5,12},... | collective-permute-start | bytes 3072008 | tf_op jit(solution)/shard_map/ppermute | solution.py:181
  15.2 24.0 %all_gather.9 = bf16[4,32,640]{2,1,0:T(8,128)(2,1)S(1)} all-gather(bf16[1,32,640]{2,1,0:T(8,128)(2,1)S(1)} %copy-done.4), channel_id=1, replica_groups=mesh['za'=4,'zb'=4,'core'=2,'xh'=2,'y'=4,'xl'=2] {'za'}, dimensions={0}, use_global_device_ids=true | all-gather | bytes 204800 | tf_op jit(solution)/shard_map/all_gather | solution.py:183
  39.2 13.7 %all-gather = bf16[16,32,640]{2,1,0:T(8,128)(2,1)S(1)} all-gather(bf16[4,32,640]{2,1,0:T(8,128)(2,1)S(1)} %all_gather.9), channel_id=2, replica_groups=mesh['za'=4,'zb'=4,'core'=2,'xh'=2,'y'=4,'xl'=2] {'zb'}, dimensions={0}, use_global_device_ids=true | all-gather | bytes 819200 | tf_op jit(solution)/shard_map/all_gather | solution.py:183
  52.8 7.7 %collective-permute-start.1 = (bf16[4,4,32,640]{3,2,1,0:T(8,128)(2,1)S(1)}, bf16[4,4,32,640]{3,2,1,0:T(8,128)(2,1)}, u32[]{:S(2)}, u32[]{:S(2)}) collective-permute-start(bf16[4,4,32,640]{3,2,1,0:T(8,128)(2,1)S(1)} %bitcast.13), channel_id=1, source_target_pairs={{0,16},{16,0},{1,17},{17,1},{2,18},{18,2},{3,19},{19,3},{4,20},{20... | collective-permute-start | bytes 1966088 | tf_op jit(solution)/shard_map/ppermute | solution.py:184
  60.5 0.8 constant_dynamic-slice_fusion
  61.2 2.0 %collective-permute-start = (bf16[4,2,32,640]{3,2,1,0:T(8,128)(2,1)}, bf16[4,2,32,640]{3,2,1,0:T(8,128)(2,1)}, u32[]{:S(2)}, u32[]{:S(2)}) collective-permute-start(bf16[4,2,32,640]{3,2,1,0:T(8,128)(2,1)} %constant_dynamic-slice_fusion), channel_id=1, source_target_pairs={{0,8},{8,0},{1,9},{9,1},{2,10},{10,2},{3,11},{11,3},{4,12},{12,4},... | collective-permute-start | bytes 983048 | tf_op jit(solution)/shard_map/ppermute | solution.py:186
  63.3 0.1 stack.27.pos
  63.4 0.0 collective-permute-done.1.other
  63.4 0.0 collective-permute-done.2.far_w
  63.4 0.0 all-to-all-done.hidden
  63.4 0.0 copy-start
  63.4 1.2 copy-done
  64.6 1.4 %copy-done.1 = bf16[8,800,128]{2,1,0:T(8,128)(2,1)S(1)} copy-done((bf16[8,800,128]{2,1,0:T(8,128)(2,1)S(1)}, bf16[8,800,128]{2,1,0:T(8,128)(2,1)}, u32[]{:S(2)}) %copy-start.1) | copy-done | bytes 1638424
  66.0 3.6 %own_weight_grad.1 = (f32[800,640]{1,0:T(8,128)S(1)}, f32[2]{0:T(128)S(1)}) custom-call(s32[6]{0:T(128)S(1)} %stack.27.pos, bf16[8,800,128]{2,1,0:T(8,128)(2,1)S(1)} %copy-done.1, bf16[4,4,32,640]{3,2,1,0:T(8,128)(2,1)S(1)} %bitcast.15, bf16[4,4,32,640]{3,2,1,0:T(8,128)(2,1)} %collective-permute-done.1.other), custom_call_target="tpu_custom_call" | custom-call | flops 1048576000 | bytes 5000000 | tf_op jit(solution)/shard_map/own_weight_grad/pallas_call | solution.py:58
  69.6 8.8 %psum.7 = f32[2]{0:T(128)S(1)} all-reduce(f32[2]{0:T(128)S(1)} %get-tuple-element.20), channel_id=1, replica_groups=mesh['za'=4,'zb'=4,'core'=2,'xh'=2,'y'=4,'xl'=2] {'xh','xl'}, use_global_device_ids=true, to_apply=%region_0.0 | all-reduce | flops 2 | bytes 16 | tf_op jit(solution)/shard_map/psum | solution.py:190
  78.4 0.0 collective-permute-done.far
  78.4 1.9 %collective-permute-start.4 = (f32[800,640]{1,0:T(8,128)S(1)}, f32[800,640]{1,0:T(8,128)}, u32[]{:S(2)}, u32[]{:S(2)}) collective-permute-start(f32[800,640]{1,0:T(8,128)S(1)} %get-tuple-element.27.block), channel_id=1, source_target_pairs={{0,1},{1,0},{2,3},{3,2},{4,5},{5,4},{6,7},{7,6},{8,9},{9,8},{10,11... | collective-permute-start | bytes 6144008 | tf_op jit(solution)/shard_map/ppermute | solution.py:192
  80.3 4.2 %collective-permute-start.3 = (bf16[4,2,32,640]{3,2,1,0:T(8,128)(2,1)}, bf16[4,2,32,640]{3,2,1,0:T(8,128)(2,1)S(1)}, u32[]{:S(2)}, u32[]{:S(2)}) collective-permute-start(bf16[4,2,32,640]{3,2,1,0:T(8,128)(2,1)} %collective-permute-done.far), channel_id=1, source_target_pairs={{0,16},{16,0},{1,17},{17,1},{2,18},{18,2},{3,19},{19,3},{4,20},{20... | collective-permute-start | bytes 983048 | tf_op jit(solution)/shard_map/ppermute | solution.py:193
  84.6 1.4 %collective-permute-done.3.far_other = bf16[4,2,32,640]{3,2,1,0:T(8,128)(2,1)S(1)} collective-permute-done((bf16[4,2,32,640]{3,2,1,0:T(8,128)(2,1)}, bf16[4,2,32,640]{3,2,1,0:T(8,128)(2,1)S(1)}, u32[]{:S(2)}, u32[]{:S(2)}) %collective-permute-start.3) | collective-permute-done | bytes 327712 | tf_op jit(solution)/shard_map/ppermute | solution.py:193
  86.0 1.2 copy-done.3
  87.2 4.1 %input_grad_partials.1 = (f32[800,128]{1,0:T(8,128)S(1)}, f32[800,128]{1,0:T(8,128)}, f32[800,128]{1,0:T(8,128)}, f32[800,128]{1,0:T(8,128)}) custom-call(s32[6]{0:T(128)S(1)} %stack.27.pos, bf16[4,4,32,640]{3,2,1,0:T(8,128)(2,1)S(1)} %bitcast.16, bf16[4,4,32,640]{3,2,1,0:T(8,128)(2,1)} %collective-permute-done.1.other, ...), custom_call_target="tpu_custom_call" | custom-call | flops 1048576000 | bytes 6000000 | tf_op jit(solution)/shard_map/input_grad_partials/pallas_call | solution.py:95
  91.3 2.5 %collective-permute-start.5 = (f32[800,128]{1,0:T(8,128)}, f32[800,128]{1,0:T(8,128)S(1)}, u32[]{:S(2)}, u32[]{:S(2)}) collective-permute-start(f32[800,128]{1,0:T(8,128)} %get-tuple-element.29), channel_id=1, source_target_pairs={{0,2},{2,0},{4,6},{6,4},{1,3},{3,1},{5,7},{7,5},{8,10},{10,8},{12,... | collective-permute-start | bytes 1228808 | tf_op jit(solution)/shard_map/ppermute | solution.py:196
  93.8 4.2 %collective-permute-start.6 = (f32[800,128]{1,0:T(8,128)}, f32[800,128]{1,0:T(8,128)S(1)}, u32[]{:S(2)}, u32[]{:S(2)}) collective-permute-start(f32[800,128]{1,0:T(8,128)} %get-tuple-element.30), channel_id=1, source_target_pairs={{0,4},{2,6},{4,0},{6,2},{1,5},{3,7},{5,1},{7,3},{8,12},{10,14},{12... | collective-permute-start | bytes 1228808 | tf_op jit(solution)/shard_map/ppermute | solution.py:196
  98.0 2.9 %collective-permute-start.7 = (f32[800,128]{1,0:T(8,128)}, f32[800,128]{1,0:T(8,128)}, u32[]{:S(2)}, u32[]{:S(2)}) collective-permute-start(f32[800,128]{1,0:T(8,128)} %get-tuple-element.31), channel_id=1, source_target_pairs={{0,6},{2,4},{4,2},{6,0},{1,7},{3,5},{5,3},{7,1},{8,14},{10,12},{12... | collective-permute-start | bytes 1228808 | tf_op jit(solution)/shard_map/ppermute | solution.py:196
  100.9 26.2 %all_to_all.11 = f32[128,1,2]{2,1,0:T(1,128)S(1)} all-to-all(f32[128,1,2]{2,1,0:T(1,128)S(1)} %broadcast_in_dim.13), channel_id=1, replica_groups=mesh['za'=4,'zb'=4,'core'=2,'xh'=2,'y'=4,'xl'=2] {'za','zb','core','y'}, dimensions={0} | all-to-all | bytes 2048 | tf_op jit(solution)/shard_map/all_to_all | solution.py:199
  127.1 0.2 reduce_sum.9.squared
  127.3 0.0 collective-permute-done.5.q1
  127.3 0.0 collective-permute-done.6.q2
  127.3 0.0 collective-permute-done.7.q3
  127.3 5.0 %combine.1 = (f32[800,640]{1,0:T(8,128)}, bf16[800,128]{1,0:T(8,128)(2,1)}, f32[1]{0:T(128)}) custom-call(s32[6]{0:T(128)S(1)} %stack.27.pos, f32[2]{0:T(128)S(1)} %reduce_sum.9.squared, f32[800,640]{1,0:T(8,128)S(1)} %get-tuple-element.27.block, f32[800,640]{1,0:T(8,128)} %collective-permute-done.4.peer, f32[800,128]{1,0:T(8,128)S(1)} %get-tuple-element.28.q0, ...), custom_call_target="tpu_custom_call" | custom-call | flops 1536000 | bytes 8000000 | tf_op jit(solution)/shard_map/combine/pallas_call | solution.py:149
  (8 shorter events, 0.0 us)
Async XLA Ops:
  2.9 7.6 %copy-start.2 = (bf16[800,640]{1,0:T(8,128)(2,1)S(1)}, bf16[800,640]{1,0:T(8,128)(2,1)}, u32[]{:S(2)}) copy-start(bf16[800,640]{1,0:T(8,128)(2,1)} %w.1) | copy-start | bytes 3072004
  2.9 12.2 %copy-start.4 = (bf16[1,32,640]{2,1,0:T(8,128)(2,1)S(1)}, bf16[1,32,640]{2,1,0:T(8,128)(2,1)}, u32[]{:S(2)}) copy-start(bf16[1,32,640]{2,1,0:T(8,128)(2,1)} %param.4) | copy-start | bytes 122884
  2.9 60.4 %all-to-all-start = ((bf16[8,800,128]{2,1,0:T(8,128)(2,1)}), bf16[8,800,128]{2,1,0:T(8,128)(2,1)S(1)}, u32[]{:S(2)}, u32[]{:S(2)}) async-start(bf16[8,800,128]{2,1,0:T(8,128)(2,1)} %broadcast_in_dim.12), calls=%async_computation | async-start | bytes 3276800 | tf_op jit(solution)/shard_map/all_to_all | solution.py:178
  10.6 52.8 %collective-permute-start.2 = (bf16[800,640]{1,0:T(8,128)(2,1)S(1)}, bf16[800,640]{1,0:T(8,128)(2,1)}, u32[]{:S(2)}, u32[]{:S(2)}) collective-permute-start(bf16[800,640]{1,0:T(8,128)(2,1)S(1)} %copy-done.2), channel_id=1, source_target_pairs={{0,9},{1,8},{8,1},{9,0},{2,11},{3,10},{10,3},{11,2},{4,13},{5,12},... | collective-permute-start | bytes 3072008 | tf_op jit(solution)/shard_map/ppermute | solution.py:181
  52.8 10.6 %collective-permute-start.1 = (bf16[4,4,32,640]{3,2,1,0:T(8,128)(2,1)S(1)}, bf16[4,4,32,640]{3,2,1,0:T(8,128)(2,1)}, u32[]{:S(2)}, u32[]{:S(2)}) collective-permute-start(bf16[4,4,32,640]{3,2,1,0:T(8,128)(2,1)S(1)} %bitcast.13), channel_id=1, source_target_pairs={{0,16},{16,0},{1,17},{17,1},{2,18},{18,2},{3,19},{19,3},{4,20},{20... | collective-permute-start | bytes 1966088 | tf_op jit(solution)/shard_map/ppermute | solution.py:184
  61.2 17.2 %collective-permute-start = (bf16[4,2,32,640]{3,2,1,0:T(8,128)(2,1)}, bf16[4,2,32,640]{3,2,1,0:T(8,128)(2,1)}, u32[]{:S(2)}, u32[]{:S(2)}) collective-permute-start(bf16[4,2,32,640]{3,2,1,0:T(8,128)(2,1)} %constant_dynamic-slice_fusion), channel_id=1, source_target_pairs={{0,8},{8,0},{1,9},{9,1},{2,10},{10,2},{3,11},{11,3},{4,12},{12,4},... | collective-permute-start | bytes 983048 | tf_op jit(solution)/shard_map/ppermute | solution.py:186
  63.4 1.2 copy-start
  64.6 1.4 %copy-start.1 = (bf16[8,800,128]{2,1,0:T(8,128)(2,1)S(1)}, bf16[8,800,128]{2,1,0:T(8,128)(2,1)}, u32[]{:S(2)}) copy-start(bf16[8,800,128]{2,1,0:T(8,128)(2,1)} %copy-done) | copy-start | bytes 4915204
  78.4 48.9 %collective-permute-start.4 = (f32[800,640]{1,0:T(8,128)S(1)}, f32[800,640]{1,0:T(8,128)}, u32[]{:S(2)}, u32[]{:S(2)}) collective-permute-start(f32[800,640]{1,0:T(8,128)S(1)} %get-tuple-element.27.block), channel_id=1, source_target_pairs={{0,1},{1,0},{2,3},{3,2},{4,5},{5,4},{6,7},{7,6},{8,9},{9,8},{10,11... | collective-permute-start | bytes 6144008 | tf_op jit(solution)/shard_map/ppermute | solution.py:192
  80.3 5.7 %collective-permute-start.3 = (bf16[4,2,32,640]{3,2,1,0:T(8,128)(2,1)}, bf16[4,2,32,640]{3,2,1,0:T(8,128)(2,1)S(1)}, u32[]{:S(2)}, u32[]{:S(2)}) collective-permute-start(bf16[4,2,32,640]{3,2,1,0:T(8,128)(2,1)} %collective-permute-done.far), channel_id=1, source_target_pairs={{0,16},{16,0},{1,17},{17,1},{2,18},{18,2},{3,19},{19,3},{4,20},{20... | collective-permute-start | bytes 983048 | tf_op jit(solution)/shard_map/ppermute | solution.py:193
  86.0 1.2 copy-start.3
  91.3 36.0 %collective-permute-start.5 = (f32[800,128]{1,0:T(8,128)}, f32[800,128]{1,0:T(8,128)S(1)}, u32[]{:S(2)}, u32[]{:S(2)}) collective-permute-start(f32[800,128]{1,0:T(8,128)} %get-tuple-element.29), channel_id=1, source_target_pairs={{0,2},{2,0},{4,6},{6,4},{1,3},{3,1},{5,7},{7,5},{8,10},{10,8},{12,... | collective-permute-start | bytes 1228808 | tf_op jit(solution)/shard_map/ppermute | solution.py:196
  93.8 33.5 %collective-permute-start.6 = (f32[800,128]{1,0:T(8,128)}, f32[800,128]{1,0:T(8,128)S(1)}, u32[]{:S(2)}, u32[]{:S(2)}) collective-permute-start(f32[800,128]{1,0:T(8,128)} %get-tuple-element.30), channel_id=1, source_target_pairs={{0,4},{2,6},{4,0},{6,2},{1,5},{3,7},{5,1},{7,3},{8,12},{10,14},{12... | collective-permute-start | bytes 1228808 | tf_op jit(solution)/shard_map/ppermute | solution.py:196
  98.0 29.3 %collective-permute-start.7 = (f32[800,128]{1,0:T(8,128)}, f32[800,128]{1,0:T(8,128)}, u32[]{:S(2)}, u32[]{:S(2)}) collective-permute-start(f32[800,128]{1,0:T(8,128)} %get-tuple-element.31), channel_id=1, source_target_pairs={{0,6},{2,4},{4,2},{6,0},{1,7},{3,5},{5,3},{7,1},{8,14},{10,12},{12... | collective-permute-start | bytes 1228808 | tf_op jit(solution)/shard_map/ppermute | solution.py:196

commit v4 on v3

--- a/solution.py
+++ b/solution.py
@@ -109,7 +109,7 @@
     )(pos, mine, other, far, far_other, weight, far_weight)
 
 
-CHUNKS = 5
+CHUNKS = 10
 ROWS = F_LOC // CHUNKS
 
 
@@ -121,9 +121,10 @@
         b_buf, p_buf, o_buf, q_buf, sems, out_sems,
     ):
         rows = [pl.ds(i * ROWS, ROWS) for i in range(CHUNKS)]
-        pairs = [(q, q_buf.at[i]) for i, q in enumerate((q0, q1, q2, q3))]
+        pairs = []
         for r in rows:
             pairs += [(block.at[r], b_buf.at[r]), (peer.at[r], p_buf.at[r])]
+        pairs += [(q, q_buf.at[i]) for i, q in enumerate((q0, q1, q2, q3))]
         copies = fetch(pairs, sems)
         xl = pos[5]
         norms = [jnp.sqrt(jnp.full((8, D_LOC), squared[i], F32)) for i in range(2)]
@@ -131,17 +132,17 @@
         own = jnp.where(xl == 0, factors[0], factors[1])
         next_ = jnp.where(xl == 0, factors[1], factors[0])
         norm[0] = jnp.max(jnp.where(xl == 0, norms[0], norms[1]))
-        for copy in copies[:4]:
-            copy.wait()
-        tokens[...] = (q_buf[0] + q_buf[1] + q_buf[2] + q_buf[3]).astype(BF16)
         stores = []
         for i, r in enumerate(rows):
-            copies[4 + 2 * i].wait()
-            copies[5 + 2 * i].wait()
+            copies[2 * i].wait()
+            copies[2 * i + 1].wait()
             o_buf[r] = own * b_buf[r] + next_ * p_buf[r]
             store = pltpu.make_async_copy(o_buf.at[r], out.at[r], out_sems.at[i])
             store.start()
             stores.append(store)
+        for copy in copies[2 * CHUNKS :]:
+            copy.wait()
+        tokens[...] = (q_buf[0] + q_buf[1] + q_buf[2] + q_buf[3]).astype(BF16)
         for store in stores:
             store.wait()
 

time: 133 us -> 134 us (level)
  no operation moved by 1% of the time
where the time goes in v4:
time: 134 us; the launch traced here: 133 us
  blocking collectives  72.6 us (54%)
  starting transfers between devices  37.6 us (28%)
  Pallas kernels  13.9 us (10%)
  local copies, waits for them, and re-layouts  6.99 us (5%)
  waiting for transfers between devices  1.47 us (1%)
    all_gather x2, blocking collectives, local(): mine = lax.all_gather(lax.all_gather(out_grads[0], 'za'), 'zb')  37.6 us
    all_to_all x1, blocking collectives, local(): lax.all_to_all(spread, ('za', 'zb', 'core', 'y'), 0, 0)  26.2 us
    ppermute x3, starting transfers between devices, local(): got = [lax.ppermute(p, 'y', flip(4, k)) for k, p in zip((1, 2, 3), parts)]  9.57 us
    psum x1, blocking collectives, local(): squared = lax.psum(squared, ('xh', 'xl'))  8.81 us
    ppermute x1, starting transfers between devices, local(): other = lax.ppermute(mine, 'core', flip(2, 1))  7.66 us
    all_to_all x1, starting transfers between devices, local(): lax.all_to_all(jnp.broadcast_to(activations[0].T[None], (8, F_LOC, 128)),...  7.61 us
    pallas_call x1, Pallas kernels, combine(): pl.pallas_call(body, out_shape=(jax.ShapeDtypeStruct((F_LOC, D_LOC), F32)...  6.18 us
    ppermute x1, starting transfers between devices, local(): lax.ppermute(weight, ('xh', 'xl'), [(i, 3 - i) for i in range(4)])  4.6 us
  transfers between devices with their start and end apart: 9, of which 1 were waited for; matrix products, arithmetic and copies ran while one was open for 1% of the time, Pallas kernels for 6%

profile of v4, /device:TPU:1, one launch (start us, length us, event | category | flops | bytes accessed | tf_op | source)
XLA Modules:
  0.0 133.5 jit_solution(10725804061499255690)
XLA Ops:
  0.6 2.3 %broadcast_in_dim.12 = bf16[8,800,128]{2,1,0:T(8,128)(2,1)} broadcast(bf16[800,128]{1,0:T(8,128)(2,1)} %bitcast.17), dimensions={1,2} | broadcast | bytes 1843200 | tf_op jit(solution)/shard_map/broadcast_in_dim | solution.py:180
  2.9 7.6 %all-to-all-start = ((bf16[8,800,128]{2,1,0:T(8,128)(2,1)}), bf16[8,800,128]{2,1,0:T(8,128)(2,1)S(1)}, u32[]{:S(2)}, u32[]{:S(2)}) async-start(bf16[8,800,128]{2,1,0:T(8,128)(2,1)} %broadcast_in_dim.12), calls=%async_computation | async-start | bytes 3276800 | tf_op jit(solution)/shard_map/all_to_all | solution.py:179
  10.6 4.6 %collective-permute-start.2 = (bf16[800,640]{1,0:T(8,128)(2,1)S(1)}, bf16[800,640]{1,0:T(8,128)(2,1)}, u32[]{:S(2)}, u32[]{:S(2)}) collective-permute-start(bf16[800,640]{1,0:T(8,128)(2,1)S(1)} %copy-done.2), channel_id=1, source_target_pairs={{0,9},{1,8},{8,1},{9,0},{2,11},{3,10},{10,3},{11,2},{4,13},{5,12},... | collective-permute-start | bytes 3072008 | tf_op jit(solution)/shard_map/ppermute | solution.py:182
  15.2 24.0 %all_gather.9 = bf16[4,32,640]{2,1,0:T(8,128)(2,1)S(1)} all-gather(bf16[1,32,640]{2,1,0:T(8,128)(2,1)S(1)} %copy-done.4), channel_id=1, replica_groups=mesh['za'=4,'zb'=4,'core'=2,'xh'=2,'y'=4,'xl'=2] {'za'}, dimensions={0}, use_global_device_ids=true | all-gather | bytes 204800 | tf_op jit(solution)/shard_map/all_gather | solution.py:184
  39.2 13.7 %all-gather = bf16[16,32,640]{2,1,0:T(8,128)(2,1)S(1)} all-gather(bf16[4,32,640]{2,1,0:T(8,128)(2,1)S(1)} %all_gather.9), channel_id=2, replica_groups=mesh['za'=4,'zb'=4,'core'=2,'xh'=2,'y'=4,'xl'=2] {'zb'}, dimensions={0}, use_global_device_ids=true | all-gather | bytes 819200 | tf_op jit(solution)/shard_map/all_gather | solution.py:184
  52.8 7.7 %collective-permute-start.1 = (bf16[4,4,32,640]{3,2,1,0:T(8,128)(2,1)S(1)}, bf16[4,4,32,640]{3,2,1,0:T(8,128)(2,1)}, u32[]{:S(2)}, u32[]{:S(2)}) collective-permute-start(bf16[4,4,32,640]{3,2,1,0:T(8,128)(2,1)S(1)} %bitcast.13), channel_id=1, source_target_pairs={{0,16},{16,0},{1,17},{17,1},{2,18},{18,2},{3,19},{19,3},{4,20},{20... | collective-permute-start | bytes 1966088 | tf_op jit(solution)/shard_map/ppermute | solution.py:185
  60.5 0.8 constant_dynamic-slice_fusion
  61.2 2.0 %collective-permute-start = (bf16[4,2,32,640]{3,2,1,0:T(8,128)(2,1)}, bf16[4,2,32,640]{3,2,1,0:T(8,128)(2,1)}, u32[]{:S(2)}, u32[]{:S(2)}) collective-permute-start(bf16[4,2,32,640]{3,2,1,0:T(8,128)(2,1)} %constant_dynamic-slice_fusion), channel_id=1, source_target_pairs={{0,8},{8,0},{1,9},{9,1},{2,10},{10,2},{3,11},{11,3},{4,12},{12,4},... | collective-permute-start | bytes 983048 | tf_op jit(solution)/shard_map/ppermute | solution.py:187
  63.3 0.1 stack.27.pos
  63.4 0.0 collective-permute-done.1.other
  63.4 0.0 collective-permute-done.2.far_w
  63.4 0.0 all-to-all-done.hidden
  63.4 0.0 copy-start
  63.4 1.2 copy-done
  64.6 1.4 %copy-done.1 = bf16[8,800,128]{2,1,0:T(8,128)(2,1)S(1)} copy-done((bf16[8,800,128]{2,1,0:T(8,128)(2,1)S(1)}, bf16[8,800,128]{2,1,0:T(8,128)(2,1)}, u32[]{:S(2)}) %copy-start.1) | copy-done | bytes 1638424
  66.0 3.6 %own_weight_grad.1 = (f32[800,640]{1,0:T(8,128)S(1)}, f32[2]{0:T(128)S(1)}) custom-call(s32[6]{0:T(128)S(1)} %stack.27.pos, bf16[8,800,128]{2,1,0:T(8,128)(2,1)S(1)} %copy-done.1, bf16[4,4,32,640]{3,2,1,0:T(8,128)(2,1)S(1)} %bitcast.15, bf16[4,4,32,640]{3,2,1,0:T(8,128)(2,1)} %collective-permute-done.1.other), custom_call_target="tpu_custom_call" | custom-call | flops 1048576000 | bytes 5000000 | tf_op jit(solution)/shard_map/own_weight_grad/pallas_call | solution.py:58
  69.6 8.8 %psum.7 = f32[2]{0:T(128)S(1)} all-reduce(f32[2]{0:T(128)S(1)} %get-tuple-element.20), channel_id=1, replica_groups=mesh['za'=4,'zb'=4,'core'=2,'xh'=2,'y'=4,'xl'=2] {'xh','xl'}, use_global_device_ids=true, to_apply=%region_0.0 | all-reduce | flops 2 | bytes 16 | tf_op jit(solution)/shard_map/psum | solution.py:191
  78.4 0.0 collective-permute-done.far
  78.4 1.9 %collective-permute-start.4 = (f32[800,640]{1,0:T(8,128)S(1)}, f32[800,640]{1,0:T(8,128)}, u32[]{:S(2)}, u32[]{:S(2)}) collective-permute-start(f32[800,640]{1,0:T(8,128)S(1)} %get-tuple-element.27.block), channel_id=1, source_target_pairs={{0,1},{1,0},{2,3},{3,2},{4,5},{5,4},{6,7},{7,6},{8,9},{9,8},{10,11... | collective-permute-start | bytes 6144008 | tf_op jit(solution)/shard_map/ppermute | solution.py:193
  80.3 4.2 %collective-permute-start.3 = (bf16[4,2,32,640]{3,2,1,0:T(8,128)(2,1)}, bf16[4,2,32,640]{3,2,1,0:T(8,128)(2,1)S(1)}, u32[]{:S(2)}, u32[]{:S(2)}) collective-permute-start(bf16[4,2,32,640]{3,2,1,0:T(8,128)(2,1)} %collective-permute-done.far), channel_id=1, source_target_pairs={{0,16},{16,0},{1,17},{17,1},{2,18},{18,2},{3,19},{19,3},{4,20},{20... | collective-permute-start | bytes 983048 | tf_op jit(solution)/shard_map/ppermute | solution.py:194
  84.6 1.4 %collective-permute-done.3.far_other = bf16[4,2,32,640]{3,2,1,0:T(8,128)(2,1)S(1)} collective-permute-done((bf16[4,2,32,640]{3,2,1,0:T(8,128)(2,1)}, bf16[4,2,32,640]{3,2,1,0:T(8,128)(2,1)S(1)}, u32[]{:S(2)}, u32[]{:S(2)}) %collective-permute-start.3) | collective-permute-done | bytes 327712 | tf_op jit(solution)/shard_map/ppermute | solution.py:194
  86.0 1.2 copy-done.3
  87.2 4.1 %input_grad_partials.1 = (f32[800,128]{1,0:T(8,128)S(1)}, f32[800,128]{1,0:T(8,128)}, f32[800,128]{1,0:T(8,128)}, f32[800,128]{1,0:T(8,128)}) custom-call(s32[6]{0:T(128)S(1)} %stack.27.pos, bf16[4,4,32,640]{3,2,1,0:T(8,128)(2,1)S(1)} %bitcast.16, bf16[4,4,32,640]{3,2,1,0:T(8,128)(2,1)} %collective-permute-done.1.other, ...), custom_call_target="tpu_custom_call" | custom-call | flops 1048576000 | bytes 6000000 | tf_op jit(solution)/shard_map/input_grad_partials/pallas_call | solution.py:95
  91.3 2.5 %collective-permute-start.5 = (f32[800,128]{1,0:T(8,128)}, f32[800,128]{1,0:T(8,128)S(1)}, u32[]{:S(2)}, u32[]{:S(2)}) collective-permute-start(f32[800,128]{1,0:T(8,128)} %get-tuple-element.29), channel_id=1, source_target_pairs={{0,2},{2,0},{4,6},{6,4},{1,3},{3,1},{5,7},{7,5},{8,10},{10,8},{12,... | collective-permute-start | bytes 1228808 | tf_op jit(solution)/shard_map/ppermute | solution.py:197
  93.8 4.2 %collective-permute-start.6 = (f32[800,128]{1,0:T(8,128)}, f32[800,128]{1,0:T(8,128)S(1)}, u32[]{:S(2)}, u32[]{:S(2)}) collective-permute-start(f32[800,128]{1,0:T(8,128)} %get-tuple-element.30), channel_id=1, source_target_pairs={{0,4},{2,6},{4,0},{6,2},{1,5},{3,7},{5,1},{7,3},{8,12},{10,14},{12... | collective-permute-start | bytes 1228808 | tf_op jit(solution)/shard_map/ppermute | solution.py:197
  98.0 2.9 %collective-permute-start.7 = (f32[800,128]{1,0:T(8,128)}, f32[800,128]{1,0:T(8,128)}, u32[]{:S(2)}, u32[]{:S(2)}) collective-permute-start(f32[800,128]{1,0:T(8,128)} %get-tuple-element.31), channel_id=1, source_target_pairs={{0,6},{2,4},{4,2},{6,0},{1,7},{3,5},{5,3},{7,1},{8,14},{10,12},{12... | collective-permute-start | bytes 1228808 | tf_op jit(solution)/shard_map/ppermute | solution.py:197
  100.9 26.2 %all_to_all.11 = f32[128,1,2]{2,1,0:T(1,128)S(1)} all-to-all(f32[128,1,2]{2,1,0:T(1,128)S(1)} %broadcast_in_dim.13), channel_id=1, replica_groups=mesh['za'=4,'zb'=4,'core'=2,'xh'=2,'y'=4,'xl'=2] {'za','zb','core','y'}, dimensions={0} | all-to-all | bytes 2048 | tf_op jit(solution)/shard_map/all_to_all | solution.py:200
  127.1 0.2 reduce_sum.9.squared
  127.3 0.0 collective-permute-done.5.q1
  127.3 0.0 collective-permute-done.6.q2
  127.3 0.0 collective-permute-done.7.q3
  127.3 6.2 %combine.1 = (f32[800,640]{1,0:T(8,128)}, bf16[800,128]{1,0:T(8,128)(2,1)}, f32[1]{0:T(128)}) custom-call(s32[6]{0:T(128)S(1)} %stack.27.pos, f32[2]{0:T(128)S(1)} %reduce_sum.9.squared, f32[800,640]{1,0:T(8,128)S(1)} %get-tuple-element.27.block, f32[800,640]{1,0:T(8,128)} %collective-permute-done.4.peer, f32[800,128]{1,0:T(8,128)S(1)} %get-tuple-element.28.q0, ...), custom_call_target="tpu_custom_call" | custom-call | flops 1536000 | bytes 8000000 | tf_op jit(solution)/shard_map/combine/pallas_call | solution.py:150
  (8 shorter events, 0.0 us)
Async XLA Ops:
  2.9 7.6 %copy-start.2 = (bf16[800,640]{1,0:T(8,128)(2,1)S(1)}, bf16[800,640]{1,0:T(8,128)(2,1)}, u32[]{:S(2)}) copy-start(bf16[800,640]{1,0:T(8,128)(2,1)} %w.1) | copy-start | bytes 3072004
  2.9 12.2 %copy-start.4 = (bf16[1,32,640]{2,1,0:T(8,128)(2,1)S(1)}, bf16[1,32,640]{2,1,0:T(8,128)(2,1)}, u32[]{:S(2)}) copy-start(bf16[1,32,640]{2,1,0:T(8,128)(2,1)} %param.4) | copy-start | bytes 122884
  2.9 60.4 %all-to-all-start = ((bf16[8,800,128]{2,1,0:T(8,128)(2,1)}), bf16[8,800,128]{2,1,0:T(8,128)(2,1)S(1)}, u32[]{:S(2)}, u32[]{:S(2)}) async-start(bf16[8,800,128]{2,1,0:T(8,128)(2,1)} %broadcast_in_dim.12), calls=%async_computation | async-start | bytes 3276800 | tf_op jit(solution)/shard_map/all_to_all | solution.py:179
  10.6 52.8 %collective-permute-start.2 = (bf16[800,640]{1,0:T(8,128)(2,1)S(1)}, bf16[800,640]{1,0:T(8,128)(2,1)}, u32[]{:S(2)}, u32[]{:S(2)}) collective-permute-start(bf16[800,640]{1,0:T(8,128)(2,1)S(1)} %copy-done.2), channel_id=1, source_target_pairs={{0,9},{1,8},{8,1},{9,0},{2,11},{3,10},{10,3},{11,2},{4,13},{5,12},... | collective-permute-start | bytes 3072008 | tf_op jit(solution)/shard_map/ppermute | solution.py:182
  52.8 10.6 %collective-permute-start.1 = (bf16[4,4,32,640]{3,2,1,0:T(8,128)(2,1)S(1)}, bf16[4,4,32,640]{3,2,1,0:T(8,128)(2,1)}, u32[]{:S(2)}, u32[]{:S(2)}) collective-permute-start(bf16[4,4,32,640]{3,2,1,0:T(8,128)(2,1)S(1)} %bitcast.13), channel_id=1, source_target_pairs={{0,16},{16,0},{1,17},{17,1},{2,18},{18,2},{3,19},{19,3},{4,20},{20... | collective-permute-start | bytes 1966088 | tf_op jit(solution)/shard_map/ppermute | solution.py:185
  61.2 17.2 %collective-permute-start = (bf16[4,2,32,640]{3,2,1,0:T(8,128)(2,1)}, bf16[4,2,32,640]{3,2,1,0:T(8,128)(2,1)}, u32[]{:S(2)}, u32[]{:S(2)}) collective-permute-start(bf16[4,2,32,640]{3,2,1,0:T(8,128)(2,1)} %constant_dynamic-slice_fusion), channel_id=1, source_target_pairs={{0,8},{8,0},{1,9},{9,1},{2,10},{10,2},{3,11},{11,3},{4,12},{12,4},... | collective-permute-start | bytes 983048 | tf_op jit(solution)/shard_map/ppermute | solution.py:187
  63.4 1.2 copy-start
  64.6 1.4 %copy-start.1 = (bf16[8,800,128]{2,1,0:T(8,128)(2,1)S(1)}, bf16[8,800,128]{2,1,0:T(8,128)(2,1)}, u32[]{:S(2)}) copy-start(bf16[8,800,128]{2,1,0:T(8,128)(2,1)} %copy-done) | copy-start | bytes 4915204
  78.4 48.9 %collective-permute-start.4 = (f32[800,640]{1,0:T(8,128)S(1)}, f32[800,640]{1,0:T(8,128)}, u32[]{:S(2)}, u32[]{:S(2)}) collective-permute-start(f32[800,640]{1,0:T(8,128)S(1)} %get-tuple-element.27.block), channel_id=1, source_target_pairs={{0,1},{1,0},{2,3},{3,2},{4,5},{5,4},{6,7},{7,6},{8,9},{9,8},{10,11... | collective-permute-start | bytes 6144008 | tf_op jit(solution)/shard_map/ppermute | solution.py:193
  80.3 5.7 %collective-permute-start.3 = (bf16[4,2,32,640]{3,2,1,0:T(8,128)(2,1)}, bf16[4,2,32,640]{3,2,1,0:T(8,128)(2,1)S(1)}, u32[]{:S(2)}, u32[]{:S(2)}) collective-permute-start(bf16[4,2,32,640]{3,2,1,0:T(8,128)(2,1)} %collective-permute-done.far), channel_id=1, source_target_pairs={{0,16},{16,0},{1,17},{17,1},{2,18},{18,2},{3,19},{19,3},{4,20},{20... | collective-permute-start | bytes 983048 | tf_op jit(solution)/shard_map/ppermute | solution.py:194
  86.0 1.2 copy-start.3
  91.3 36.0 %collective-permute-start.5 = (f32[800,128]{1,0:T(8,128)}, f32[800,128]{1,0:T(8,128)S(1)}, u32[]{:S(2)}, u32[]{:S(2)}) collective-permute-start(f32[800,128]{1,0:T(8,128)} %get-tuple-element.29), channel_id=1, source_target_pairs={{0,2},{2,0},{4,6},{6,4},{1,3},{3,1},{5,7},{7,5},{8,10},{10,8},{12,... | collective-permute-start | bytes 1228808 | tf_op jit(solution)/shard_map/ppermute | solution.py:197
  93.8 33.5 %collective-permute-start.6 = (f32[800,128]{1,0:T(8,128)}, f32[800,128]{1,0:T(8,128)S(1)}, u32[]{:S(2)}, u32[]{:S(2)}) collective-permute-start(f32[800,128]{1,0:T(8,128)} %get-tuple-element.30), channel_id=1, source_target_pairs={{0,4},{2,6},{4,0},{6,2},{1,5},{3,7},{5,1},{7,3},{8,12},{10,14},{12... | collective-permute-start | bytes 1228808 | tf_op jit(solution)/shard_map/ppermute | solution.py:197
  98.0 29.3 %collective-permute-start.7 = (f32[800,128]{1,0:T(8,128)}, f32[800,128]{1,0:T(8,128)}, u32[]{:S(2)}, u32[]{:S(2)}) collective-permute-start(f32[800,128]{1,0:T(8,128)} %get-tuple-element.31), channel_id=1, source_target_pairs={{0,6},{2,4},{4,2},{6,0},{1,7},{3,5},{5,3},{7,1},{8,14},{10,12},{12... | collective-permute-start | bytes 1228808 | tf_op jit(solution)/shard_map/ppermute | solution.py:197
